TPU v7x, 32 devices: a whole 2x2x4 slice. The times are simulated.
32 devices in a mesh: dp: 8 (over z, x), rep: 4 (over y, core).
Axes of the slice: x: 2, y: 2, z: 4, core: 2. Of those that a mesh axis runs over, the one named last changes fastest.
Arguments:
- input_160: bfloat16 [128, 10, 10, 1024], P(('dp', 'rep')), may hold values from -6 to 6
- input_224: bfloat16 [64, 14, 14, 1024], P(('dp', 'rep')), may hold values from -6 to 6
- input_288: bfloat16 [64, 18, 18, 1024], P(('dp', 'rep')), may hold values from -6 to 6
- cotangent_160: bfloat16 [128, 5, 5, 2048], P(('dp', 'rep')), may hold values from -6 to 6
- cotangent_224: bfloat16 [64, 7, 7, 2048], P(('dp', 'rep')), may hold values from -6 to 6
- cotangent_288: bfloat16 [64, 9, 9, 2048], P(('dp', 'rep')), may hold values from -6 to 6
- live_counts: int32 [32, 3], P(('dp', 'rep')), may hold values from 1 to 4, as said below
- conv_a1: bfloat16 [1024, 512], P(None, 'dp'), may hold values from -0.1875 to 0.1875
- norm_a1: bfloat16 [2, 512], P(None, 'dp')
- conv_a2: bfloat16 [3, 3, 512, 512], P(None, None, None, 'dp'), may hold values from -0.09375 to 0.09375
- norm_a2: bfloat16 [2, 512], P(None, 'dp')
- conv_a3: bfloat16 [512, 2048], P(None, 'dp'), may hold values from -0.25 to 0.25
- norm_a3: bfloat16 [2, 2048], P(None, 'dp')
- conv_as: bfloat16 [1024, 2048], P(None, 'dp'), may hold values from -0.1875 to 0.1875
- norm_as: bfloat16 [2, 2048], P(None, 'dp')
- conv_b1: bfloat16 [2048, 512], P(None, 'dp'), may hold values from -0.125 to 0.125
- norm_b1: bfloat16 [2, 512], P(None, 'dp')
- conv_b2: bfloat16 [3, 3, 512, 512], P(None, None, None, 'dp'), may hold values from -0.09375 to 0.09375
- norm_b2: bfloat16 [2, 512], P(None, 'dp')
- conv_b3: bfloat16 [512, 2048], P(None, 'dp'), may hold values from -0.25 to 0.25
- norm_b3: bfloat16 [2, 2048], P(None, 'dp')
Outputs:
- output_160: bfloat16 [128, 5, 5, 2048], P(('dp', 'rep'))
- output_224: bfloat16 [64, 7, 7, 2048], P(('dp', 'rep'))
- output_288: bfloat16 [64, 9, 9, 2048], P(('dp', 'rep'))
- grad_input_160: bfloat16 [128, 10, 10, 1024], P(('dp', 'rep'))
- grad_input_224: bfloat16 [64, 14, 14, 1024], P(('dp', 'rep'))
- grad_input_288: bfloat16 [64, 18, 18, 1024], P(('dp', 'rep'))
- grad_conv_a1: float32 [1024, 512], P(None, 'dp')
- grad_norm_a1: float32 [2, 512], P(None, 'dp')
- grad_conv_a2: float32 [3, 3, 512, 512], P(None, None, None, 'dp')
- grad_norm_a2: float32 [2, 512], P(None, 'dp')
- grad_conv_a3: float32 [512, 2048], P(None, 'dp')
- grad_norm_a3: float32 [2, 2048], P(None, 'dp')
- grad_conv_as: float32 [1024, 2048], P(None, 'dp')
- grad_norm_as: float32 [2, 2048], P(None, 'dp')
- grad_conv_b1: float32 [2048, 512], P(None, 'dp')
- grad_norm_b1: float32 [2, 512], P(None, 'dp')
- grad_conv_b2: float32 [3, 3, 512, 512], P(None, None, None, 'dp')
- grad_norm_b2: float32 [2, 512], P(None, 'dp')
- grad_conv_b3: float32 [512, 2048], P(None, 'dp')
- grad_norm_b3: float32 [2, 2048], P(None, 'dp')
- lars_conv_a1: float32 [1024, 512], P(None, 'dp')
- lars_conv_a2: float32 [3, 3, 512, 512], P(None, None, None, 'dp')
- lars_conv_a3: float32 [512, 2048], P(None, 'dp')
- lars_conv_as: float32 [1024, 2048], P(None, 'dp')
- lars_conv_b1: float32 [2048, 512], P(None, 'dp')
- lars_conv_b2: float32 [3, 3, 512, 512], P(None, None, None, 'dp')
- lars_conv_b3: float32 [512, 2048], P(None, 'dp')
- norm_sums: float32 [2, 7], replicated
Inputs may be any that keep to these rules, and one draw needn't show every extreme that they name: `live_counts`: column k of a device is at least 1 and at most that group's slots on one device (4, 2, 2); in each column some device is full and some holds one image.
All inputs are finite; a program needn't handle non-finite values.
Results may differ from a plain program's by a relative error of at most 0.019.
Values may be sent and summed in bfloat16 or wider, within the bound.
A program may use at most 144 MiB of HBM per device.

v0:
```python
import jax
import jax.numpy as jnp
from jax import lax
from jax.sharding import PartitionSpec as P

EPSILON = 1e-05
DECAY_RATE = 5e-05


def silu_slope(values):
    sigmoid = jax.nn.sigmoid(values)
    return sigmoid * (1.0 + values * (1.0 - sigmoid))


def pointwise(inputs, weight):
    return jnp.einsum("nhwc,cd->nhwd", inputs, weight, preferred_element_type=jnp.float32)


def pointwise_back(upstream, weight):
    return jnp.einsum("nhwd,cd->nhwc", upstream, weight, preferred_element_type=jnp.float32)


def weight_term(inputs, upstream):
    return jnp.einsum("nhwc,nhwd->cd", inputs, upstream, preferred_element_type=jnp.float32)


def summed_terms(inputs, upstream):
    running = weight_term(inputs[0], upstream[0])
    for group_member in (1, 2):
        running = running + weight_term(inputs[group_member], upstream[group_member])
    return running


def patches(inputs, stride):
    padded = jnp.pad(inputs, ((0, 0), (1, 1), (1, 1), (0, 0)))
    extent = inputs.shape[1]
    pieces = []
    for offset_row in range(3):
        for offset_col in range(3):
            pieces.append(
                padded[
                    :,
                    offset_row : offset_row + extent : stride,
                    offset_col : offset_col + extent : stride,
                    :,
                ]
            )
    return jnp.concatenate(pieces, axis=3)


def fold_patches(upstream, stride, side_in):
    channels = upstream.shape[3] // 9
    padded = jnp.zeros((upstream.shape[0], side_in + 2, side_in + 2, channels), jnp.float32)
    for offset_row in range(3):
        for offset_col in range(3):
            start_at = (offset_row * 3 + offset_col) * channels
            padded = padded.at[
                :,
                offset_row : offset_row + side_in : stride,
                offset_col : offset_col + side_in : stride,
                :,
            ].add(upstream[..., start_at : start_at + channels])
    return padded[:, 1 : side_in + 1, 1 : side_in + 1, :]


def batch_norm(values, live_masks, norm_param, totals):
    gain_row = norm_param[0].astype(jnp.float32)
    shift_row = norm_param[1].astype(jnp.float32)
    firsts = []
    seconds = []
    for group_member in range(3):
        weighted = values[group_member] * live_masks[group_member]
        firsts.append(jnp.sum(weighted, axis=(0, 1, 2)))
        seconds.append(jnp.sum(weighted * values[group_member], axis=(0, 1, 2)))
    summed = lax.psum(
        (firsts[0], seconds[0], firsts[1], seconds[1], firsts[2], seconds[2]), ("dp", "rep")
    )
    normed = []
    means = []
    scales = []
    for group_member in range(3):
        pixel_count = (
            totals[group_member] * values[group_member].shape[1] * values[group_member].shape[2]
        )
        mean_value = summed[2 * group_member] / pixel_count
        inv_std = lax.rsqrt(
            summed[2 * group_member + 1] / pixel_count - mean_value * mean_value + EPSILON
        )
        normed.append((values[group_member] - mean_value) * inv_std * gain_row + shift_row)
        means.append(mean_value)
        scales.append(inv_std)
    return (normed, means, scales)


def norm_back(upstream, values, live_masks, norm_param, means, scales, totals):
    gain_row = norm_param[0].astype(jnp.float32)
    normals = []
    firsts = []
    seconds = []
    for group_member in range(3):
        normal = (values[group_member] - means[group_member]) * scales[group_member]
        weighted = upstream[group_member] * live_masks[group_member]
        normals.append(normal)
        firsts.append(jnp.sum(weighted, axis=(0, 1, 2)))
        seconds.append(jnp.sum(weighted * normal, axis=(0, 1, 2)))
    summed = lax.psum(
        (firsts[0], seconds[0], firsts[1], seconds[1], firsts[2], seconds[2]), ("dp", "rep")
    )
    results = []
    for group_member in range(3):
        pixel_count = (
            totals[group_member] * values[group_member].shape[1] * values[group_member].shape[2]
        )
        centered = (
            upstream[group_member]
            - summed[2 * group_member] / pixel_count
            - normals[group_member] * (summed[2 * group_member + 1] / pixel_count)
        )
        results.append(
            (live_masks[group_member] * gain_row * scales[group_member] * centered).astype(
                jnp.bfloat16
            )
        )
    param_grad = jnp.stack([summed[1] + summed[3] + summed[5], summed[0] + summed[2] + summed[4]])
    return (results, param_grad)


def own_columns(full, local_width):
    return lax.dynamic_slice_in_dim(full, lax.axis_index("dp") * local_width, local_width, 1)


def on_device(
    input_160,
    input_224,
    input_288,
    cotangent_160,
    cotangent_224,
    cotangent_288,
    live_counts,
    conv_a1,
    norm_a1,
    conv_a2,
    norm_a2,
    conv_a3,
    norm_a3,
    conv_as,
    norm_as,
    conv_b1,
    norm_b1,
    conv_b2,
    norm_b2,
    conv_b3,
    norm_b3,
):
    inputs = (input_160, input_224, input_288)
    cotangents = (cotangent_160, cotangent_224, cotangent_288)
    live_masks = []
    masked = []
    for group_member in range(3):
        group_slot_count = inputs[group_member].shape[0]
        live_flags = (
            (jnp.arange(group_slot_count) < live_counts[0, group_member])
            .astype(jnp.float32)
            .reshape(group_slot_count, 1, 1, 1)
        )
        live_masks.append(live_flags)
        masked.append(inputs[group_member] * live_flags.astype(jnp.bfloat16))
    totals = lax.psum(live_counts[0].astype(jnp.float32), ("dp", "rep"))
    local_weights = (conv_a1, conv_a2, conv_a3, conv_as, conv_b1, conv_b2, conv_b3)
    squares_list = []
    for weight in local_weights:
        squares_list.append(jnp.sum(jnp.square(weight.astype(jnp.float32))))
    weight_squares = jnp.stack(squares_list)
    gathered_a = (
        lax.all_gather(conv_a1, "dp", axis=1, tiled=True),
        lax.all_gather(norm_a1, "dp", axis=1, tiled=True),
        lax.all_gather(conv_a2, "dp", axis=3, tiled=True),
        lax.all_gather(norm_a2, "dp", axis=1, tiled=True),
        lax.all_gather(conv_a3, "dp", axis=1, tiled=True),
        lax.all_gather(norm_a3, "dp", axis=1, tiled=True),
        lax.all_gather(conv_as, "dp", axis=1, tiled=True),
        lax.all_gather(norm_as, "dp", axis=1, tiled=True),
    )
    full_a1, param_a1, full_a2, param_a2, full_a3, param_a3, full_as, param_as = gathered_a
    mid_width = full_a2.shape[3]
    out_width = full_a3.shape[1]
    hidden_a1 = [pointwise(masked[group_member], full_a1) for group_member in range(3)]
    normed_a1, means_a1, scales_a1 = batch_norm(hidden_a1, live_masks, param_a1, totals)
    act_a1 = [
        jax.nn.silu(normed_a1[group_member]).astype(jnp.bfloat16) for group_member in range(3)
    ]
    kernel_a2 = full_a2.reshape(9 * mid_width, mid_width)
    hidden_a2 = [
        pointwise(patches(act_a1[group_member], 2), kernel_a2) for group_member in range(3)
    ]
    normed_a2, means_a2, scales_a2 = batch_norm(hidden_a2, live_masks, param_a2, totals)
    act_a2 = [
        jax.nn.silu(normed_a2[group_member]).astype(jnp.bfloat16) for group_member in range(3)
    ]
    strided = [masked[group_member][:, ::2, ::2, :] for group_member in range(3)]
    joined = [
        jnp.concatenate(
            [pointwise(act_a2[group_member], full_a3), pointwise(strided[group_member], full_as)],
            axis=3,
        )
        for group_member in range(3)
    ]
    param_joined = jnp.concatenate([param_a3, param_as], axis=1)
    normed_j, means_j, scales_j = batch_norm(joined, live_masks, param_joined, totals)
    sum_a = [
        normed_j[group_member][..., :out_width] + normed_j[group_member][..., out_width:]
        for group_member in range(3)
    ]
    out_a = [
        (jax.nn.silu(sum_a[group_member]) * live_masks[group_member]).astype(jnp.bfloat16)
        for group_member in range(3)
    ]
    gathered_b = (
        lax.all_gather(conv_b1, "dp", axis=1, tiled=True),
        lax.all_gather(norm_b1, "dp", axis=1, tiled=True),
        lax.all_gather(conv_b2, "dp", axis=3, tiled=True),
        lax.all_gather(norm_b2, "dp", axis=1, tiled=True),
        lax.all_gather(conv_b3, "dp", axis=1, tiled=True),
        lax.all_gather(norm_b3, "dp", axis=1, tiled=True),
    )
    full_b1, param_b1, full_b2, param_b2, full_b3, param_b3 = gathered_b
    hidden_b1 = [pointwise(out_a[group_member], full_b1) for group_member in range(3)]
    normed_b1, means_b1, scales_b1 = batch_norm(hidden_b1, live_masks, param_b1, totals)
    act_b1 = [
        jax.nn.silu(normed_b1[group_member]).astype(jnp.bfloat16) for group_member in range(3)
    ]
    kernel_b2 = full_b2.reshape(9 * mid_width, mid_width)
    hidden_b2 = [
        pointwise(patches(act_b1[group_member], 1), kernel_b2) for group_member in range(3)
    ]
    normed_b2, means_b2, scales_b2 = batch_norm(hidden_b2, live_masks, param_b2, totals)
    act_b2 = [
        jax.nn.silu(normed_b2[group_member]).astype(jnp.bfloat16) for group_member in range(3)
    ]
    hidden_b3 = [pointwise(act_b2[group_member], full_b3) for group_member in range(3)]
    normed_b3, means_b3, scales_b3 = batch_norm(hidden_b3, live_masks, param_b3, totals)
    sum_b = [
        normed_b3[group_member] + out_a[group_member].astype(jnp.float32)
        for group_member in range(3)
    ]
    outputs = [
        (jax.nn.silu(sum_b[group_member]) * live_masks[group_member]).astype(jnp.bfloat16)
        for group_member in range(3)
    ]
    back_b = (
        lax.all_gather(conv_b1, "dp", axis=1, tiled=True),
        lax.all_gather(norm_b1, "dp", axis=1, tiled=True),
        lax.all_gather(conv_b2, "dp", axis=3, tiled=True),
        lax.all_gather(norm_b2, "dp", axis=1, tiled=True),
        lax.all_gather(conv_b3, "dp", axis=1, tiled=True),
        lax.all_gather(norm_b3, "dp", axis=1, tiled=True),
    )
    full_b1, param_b1, full_b2, param_b2, full_b3, param_b3 = back_b
    kernel_b2 = full_b2.reshape(9 * mid_width, mid_width)
    grad_sum_b = [
        cotangents[group_member].astype(jnp.float32)
        * live_masks[group_member]
        * silu_slope(sum_b[group_member])
        for group_member in range(3)
    ]
    grad_h_b3, pgrad_b3 = norm_back(
        grad_sum_b, hidden_b3, live_masks, param_b3, means_b3, scales_b3, totals
    )
    term_b3 = summed_terms(act_b2, grad_h_b3)
    grad_act = [
        pointwise_back(grad_h_b3[group_member], full_b3) * silu_slope(normed_b2[group_member])
        for group_member in range(3)
    ]
    grad_h_b2, pgrad_b2 = norm_back(
        grad_act, hidden_b2, live_masks, param_b2, means_b2, scales_b2, totals
    )
    term_b2 = summed_terms(
        [patches(act_b1[group_member], 1) for group_member in range(3)], grad_h_b2
    ).reshape(3, 3, mid_width, mid_width)
    grad_act = [
        fold_patches(
            pointwise_back(grad_h_b2[group_member], kernel_b2), 1, act_b1[group_member].shape[1]
        )
        * silu_slope(normed_b1[group_member])
        for group_member in range(3)
    ]
    grad_h_b1, pgrad_b1 = norm_back(
        grad_act, hidden_b1, live_masks, param_b1, means_b1, scales_b1, totals
    )
    term_b1 = summed_terms(out_a, grad_h_b1)
    grad_out_a = [
        grad_sum_b[group_member] + pointwise_back(grad_h_b1[group_member], full_b1)
        for group_member in range(3)
    ]
    shard_b = (
        lax.psum_scatter(term_b1, "dp", scatter_dimension=1, tiled=True),
        lax.psum_scatter(term_b2, "dp", scatter_dimension=3, tiled=True),
        lax.psum_scatter(term_b3, "dp", scatter_dimension=1, tiled=True),
    )
    grads_b = (
        lax.psum(shard_b[0].astype(jnp.bfloat16), "rep").astype(jnp.float32),
        lax.psum(shard_b[1].astype(jnp.bfloat16), "rep").astype(jnp.float32),
        lax.psum(shard_b[2].astype(jnp.bfloat16), "rep").astype(jnp.float32),
    )
    back_a = (
        lax.all_gather(conv_a1, "dp", axis=1, tiled=True),
        lax.all_gather(norm_a1, "dp", axis=1, tiled=True),
        lax.all_gather(conv_a2, "dp", axis=3, tiled=True),
        lax.all_gather(norm_a2, "dp", axis=1, tiled=True),
        lax.all_gather(conv_a3, "dp", axis=1, tiled=True),
        lax.all_gather(norm_a3, "dp", axis=1, tiled=True),
        lax.all_gather(conv_as, "dp", axis=1, tiled=True),
        lax.all_gather(norm_as, "dp", axis=1, tiled=True),
    )
    full_a1, param_a1, full_a2, param_a2, full_a3, param_a3, full_as, param_as = back_a
    kernel_a2 = full_a2.reshape(9 * mid_width, mid_width)
    param_joined = jnp.concatenate([param_a3, param_as], axis=1)
    grad_sum_a = [
        grad_out_a[group_member] * live_masks[group_member] * silu_slope(sum_a[group_member])
        for group_member in range(3)
    ]
    grad_joined = [
        jnp.concatenate([grad_sum_a[group_member], grad_sum_a[group_member]], axis=3)
        for group_member in range(3)
    ]
    grad_h_j, pgrad_j = norm_back(
        grad_joined, joined, live_masks, param_joined, means_j, scales_j, totals
    )
    grad_h_a3 = [grad_h_j[group_member][..., :out_width] for group_member in range(3)]
    grad_h_as = [grad_h_j[group_member][..., out_width:] for group_member in range(3)]
    term_a3 = summed_terms(act_a2, grad_h_a3)
    term_as = summed_terms(strided, grad_h_as)
    grad_act = [
        pointwise_back(grad_h_a3[group_member], full_a3) * silu_slope(normed_a2[group_member])
        for group_member in range(3)
    ]
    grad_h_a2, pgrad_a2 = norm_back(
        grad_act, hidden_a2, live_masks, param_a2, means_a2, scales_a2, totals
    )
    term_a2 = summed_terms(
        [patches(act_a1[group_member], 2) for group_member in range(3)], grad_h_a2
    ).reshape(3, 3, mid_width, mid_width)
    grad_act = [
        fold_patches(
            pointwise_back(grad_h_a2[group_member], kernel_a2), 2, act_a1[group_member].shape[1]
        )
        * silu_slope(normed_a1[group_member])
        for group_member in range(3)
    ]
    grad_h_a1, pgrad_a1 = norm_back(
        grad_act, hidden_a1, live_masks, param_a1, means_a1, scales_a1, totals
    )
    term_a1 = summed_terms(masked, grad_h_a1)
    grad_inputs = [
        pointwise_back(grad_h_a1[group_member], full_a1)
        .at[:, ::2, ::2, :]
        .add(pointwise_back(grad_h_as[group_member], full_as))
        .astype(jnp.bfloat16)
        for group_member in range(3)
    ]
    shard_a = (
        lax.psum_scatter(term_a1, "dp", scatter_dimension=1, tiled=True),
        lax.psum_scatter(term_a2, "dp", scatter_dimension=3, tiled=True),
        lax.psum_scatter(term_a3, "dp", scatter_dimension=1, tiled=True),
        lax.psum_scatter(term_as, "dp", scatter_dimension=1, tiled=True),
    )
    grads_a = (
        lax.psum(shard_a[0].astype(jnp.bfloat16), "rep").astype(jnp.float32),
        lax.psum(shard_a[1].astype(jnp.bfloat16), "rep").astype(jnp.float32),
        lax.psum(shard_a[2].astype(jnp.bfloat16), "rep").astype(jnp.float32),
        lax.psum(shard_a[3].astype(jnp.bfloat16), "rep").astype(jnp.float32),
    )
    mid_local = norm_a1.shape[1]
    out_local = norm_a3.shape[1]
    norm_grad_a1 = own_columns(pgrad_a1, mid_local)
    norm_grad_a2 = own_columns(pgrad_a2, mid_local)
    norm_grad_a3 = own_columns(pgrad_j[:, :out_width], out_local)
    norm_grad_as = own_columns(pgrad_j[:, out_width:], out_local)
    norm_grad_b1 = own_columns(pgrad_b1, mid_local)
    norm_grad_b2 = own_columns(pgrad_b2, mid_local)
    norm_grad_b3 = own_columns(pgrad_b3, out_local)
    gradients = (grads_a[0], grads_a[1], grads_a[2], grads_a[3], grads_b[0], grads_b[1], grads_b[2])
    grad_list = []
    for gradient in gradients:
        grad_list.append(jnp.sum(gradient * gradient))
    grad_squares = jnp.stack(grad_list)
    weight_totals, grad_totals = lax.psum((weight_squares, grad_squares), "dp")
    weight_norm = jnp.sqrt(weight_totals)
    grad_norm = jnp.sqrt(grad_totals)
    trust_ratio = weight_norm / (grad_norm + DECAY_RATE * weight_norm)
    scaled = [
        trust_ratio[layer_id]
        * (gradients[layer_id] + DECAY_RATE * local_weights[layer_id].astype(jnp.float32))
        for layer_id in range(7)
    ]
    return (
        outputs[0],
        outputs[1],
        outputs[2],
        grad_inputs[0],
        grad_inputs[1],
        grad_inputs[2],
        gradients[0],
        norm_grad_a1,
        gradients[1],
        norm_grad_a2,
        gradients[2],
        norm_grad_a3,
        gradients[3],
        norm_grad_as,
        gradients[4],
        norm_grad_b1,
        gradients[5],
        norm_grad_b2,
        gradients[6],
        norm_grad_b3,
        scaled[0],
        scaled[1],
        scaled[2],
        scaled[3],
        scaled[4],
        scaled[5],
        scaled[6],
        jnp.stack([weight_totals, grad_totals]),
    )


def solution(mesh):
    placed = (
        P(("dp", "rep"), None, None, None),
        P(("dp", "rep"), None, None, None),
        P(("dp", "rep"), None, None, None),
        P(("dp", "rep"), None, None, None),
        P(("dp", "rep"), None, None, None),
        P(("dp", "rep"), None, None, None),
        P(("dp", "rep"), None),
        P(None, "dp"),
        P(None, "dp"),
        P(None, None, None, "dp"),
        P(None, "dp"),
        P(None, "dp"),
        P(None, "dp"),
        P(None, "dp"),
        P(None, "dp"),
        P(None, "dp"),
        P(None, "dp"),
        P(None, None, None, "dp"),
        P(None, "dp"),
        P(None, "dp"),
        P(None, "dp"),
    )
    return jax.shard_map(
        on_device,
        mesh=mesh,
        in_specs=placed,
        out_specs=(
            P(("dp", "rep"), None, None, None),
            P(("dp", "rep"), None, None, None),
            P(("dp", "rep"), None, None, None),
            P(("dp", "rep"), None, None, None),
            P(("dp", "rep"), None, None, None),
            P(("dp", "rep"), None, None, None),
            P(None, "dp"),
            P(None, "dp"),
            P(None, None, None, "dp"),
            P(None, "dp"),
            P(None, "dp"),
            P(None, "dp"),
            P(None, "dp"),
            P(None, "dp"),
            P(None, "dp"),
            P(None, "dp"),
            P(None, None, None, "dp"),
            P(None, "dp"),
            P(None, "dp"),
            P(None, "dp"),
            P(None, "dp"),
            P(None, None, None, "dp"),
            P(None, "dp"),
            P(None, "dp"),
            P(None, "dp"),
            P(None, None, None, "dp"),
            P(None, "dp"),
            P(),
        ),
        check_vma=False,
    )
```

profile of v0, /device:TPU:0, one launch (start us, length us, event | category | flops | bytes accessed | tf_op | source)
XLA Modules:
  0.0 2323.5 jit_solution(4491728953930721214)
XLA Ops:
  16.5 22.1 all-gather
  38.7 16.2 all-gather.1
  62.3 5.9 slice.1507
  74.0 45.3 %all-reduce.20 = (f32[512]{0:T(512)S(1)}, f32[3]{0:T(128)S(1)}, f32[512]{0:T(512)S(1)}, f32[512]{0:T(512)S(1)}, f32[512]{0:T(512)S(1)}, /*index=5*/f32[512]{0:T(512)S(1)}, f32[512]{0:T(512)S(1)}) all-reduce(f32[512]{0:T(512)S(1)} %get-tuple-element.461, f32[3]{0:T(128)S(1)} %convert_bitcast_fusion, ...), channel_id=1, replica_groups=mesh['dp'=8,'rep'=4] {'dp','rep'}, use_global_device_ids=true, to_apply=%region_4.0 | all-reduce | flops 3075 | bytes 24600 | tf_op jit(solution)/shard_map/psum | solution.py:75
  124.1 6.2 slice.1444
  130.4 6.2 slice.1445
  136.5 6.2 slice.1446
  142.7 6.2 slice.1447
  148.9 6.2 slice.1448
  155.1 6.2 slice.1449
  161.3 6.2 slice.1450
  167.5 6.2 slice.1451
  173.7 6.2 slice.1452
  215.5 5.7 slice.1498
  221.2 5.7 slice.1499
  270.9 6.7 copy.237
  289.1 45.0 %all-reduce.19 = (f32[512]{0:T(512)S(1)}, f32[512]{0:T(512)S(1)}, f32[512]{0:T(512)S(1)}, f32[512]{0:T(512)S(1)}, f32[512]{0:T(512)S(1)}, /*index=5*/f32[512]{0:T(512)S(1)}) all-reduce(f32[512]{0:T(512)S(1)} %get-tuple-element.495, f32[512]{0:T(512)S(1)} %get-tuple-element.494, ...), channel_id=1, replica_groups=mesh['dp'=8,'rep'=4] {'dp','rep'}, use_global_device_ids=true, to_apply=%region_8.0 | all-reduce | flops 3072 | bytes 24576 | tf_op jit(solution)/shard_map/psum | solution.py:75
  351.1 19.9 all_gather.62
  371.0 16.3 all_gather.63
  387.4 18.2 all-gather.2
  405.6 16.2 all-gather.3
  422.5 18.3 all_gather.69
  445.1 6.7 copy.240
  451.8 19.2 all-reduce.29.cloned.1.call-done
  484.2 39.3 %all-gather.20.cloned.1.call-done = bf16[2048,512]{0,1:T(8,128)(2,1)} async-done(((bf16[2048,64]{0,1:T(8,128)(2,1)}), bf16[2048,512]{0,1:T(8,128)(2,1)}) %all-gather.20.cloned.1.call-update) | async-done | bytes 2097168 | tf_op jit(solution)/shard_map/all_gather | solution.py:219
  530.0 40.7 %all-reduce.17 = (f32[512]{0:T(512)S(1)}, f32[512]{0:T(512)S(1)}, f32[512]{0:T(512)S(1)}, f32[512]{0:T(512)S(1)}, f32[512]{0:T(512)S(1)}, /*index=5*/f32[512]{0:T(512)S(1)}) all-reduce(f32[512]{0:T(512)S(1)} %get-tuple-element.493, f32[512]{0:T(512)S(1)} %get-tuple-element.492, ...), channel_id=1, replica_groups=mesh['dp'=8,'rep'=4] {'dp','rep'}, use_global_device_ids=true, to_apply=%region_16.0 | all-reduce | flops 3072 | bytes 24576 | tf_op jit(solution)/shard_map/psum | solution.py:75
  583.2 41.3 %all-reduce.16 = (f32[512]{0:T(512)S(1)}, f32[512]{0:T(512)S(1)}, f32[512]{0:T(512)S(1)}, f32[512]{0:T(512)S(1)}, f32[512]{0:T(512)S(1)}, /*index=5*/f32[512]{0:T(512)S(1)}) all-reduce(f32[512]{0:T(512)S(1)} %get-tuple-element.491, f32[512]{0:T(512)S(1)} %get-tuple-element.490, ...), channel_id=1, replica_groups=mesh['dp'=8,'rep'=4] {'dp','rep'}, use_global_device_ids=true, to_apply=%region_20.21 | all-reduce | flops 3072 | bytes 24576 | tf_op jit(solution)/shard_map/psum | solution.py:75
  634.0 40.0 %all-reduce.15 = (f32[2048]{0:T(1024)S(1)}, f32[2048]{0:T(1024)S(1)}, f32[2048]{0:T(1024)S(1)}, f32[2048]{0:T(1024)S(1)}, f32[2048]{0:T(1024)S(1)}, /*index=5*/f32[2048]{0:T(1024)S(1)}) all-reduce(f32[2048]{0:T(1024)S(1)} %get-tuple-element.459, f32[2048]{0:T(1024)S(1)} %get-tuple-element.458, ...), channel_id=1, replica_groups=mesh['dp'=8,'rep'=4] {'dp','rep'}, use_global_device_ids=true, to_apply=%region_24.25 | all-reduce | flops 12288 | bytes 98304 | tf_op jit(solution)/shard_map/psum | solution.py:75
  674.3 5.2 multiply_reduce_fusion.16
  686.8 41.6 %all-reduce.14 = (f32[2048]{0:T(1024)S(1)}, f32[2048]{0:T(1024)S(1)}, f32[2048]{0:T(1024)S(1)}, f32[2048]{0:T(1024)S(1)}, f32[2048]{0:T(1024)S(1)}, /*index=5*/f32[2048]{0:T(1024)S(1)}) all-reduce(f32[2048]{0:T(1024)S(1)} %get-tuple-element.457, f32[2048]{0:T(1024)S(1)} %get-tuple-element.456, ...), channel_id=1, replica_groups=mesh['dp'=8,'rep'=4] {'dp','rep'}, use_global_device_ids=true, to_apply=%region_76.77 | all-reduce | flops 12288 | bytes 98304 | tf_op jit(solution)/shard_map/psum | solution.py:106
  741.0 39.7 %all-reduce.13 = (f32[512]{0:T(512)S(1)}, f32[512]{0:T(512)S(1)}, f32[512]{0:T(512)S(1)}, f32[512]{0:T(512)S(1)}, f32[512]{0:T(512)S(1)}, /*index=5*/f32[512]{0:T(512)S(1)}) all-reduce(f32[512]{0:T(512)S(1)} %get-tuple-element.489, f32[512]{0:T(512)S(1)} %get-tuple-element.488, ...), channel_id=1, replica_groups=mesh['dp'=8,'rep'=4] {'dp','rep'}, use_global_device_ids=true, to_apply=%region_80.81 | all-reduce | flops 3072 | bytes 24576 | tf_op jit(solution)/shard_map/psum | solution.py:106
  859.1 6.4 scatter-add.384
  869.6 6.4 scatter-add.385
  921.1 41.2 %all-reduce.12 = (f32[512]{0:T(512)S(1)}, f32[512]{0:T(512)S(1)}, f32[512]{0:T(512)S(1)}, f32[512]{0:T(512)S(1)}, f32[512]{0:T(512)S(1)}, /*index=5*/f32[512]{0:T(512)S(1)}) all-reduce(f32[512]{0:T(512)S(1)} %get-tuple-element.487, f32[512]{0:T(512)S(1)} %get-tuple-element.486, ...), channel_id=1, replica_groups=mesh['dp'=8,'rep'=4] {'dp','rep'}, use_global_device_ids=true, to_apply=%region_85.86 | all-reduce | flops 3072 | bytes 24576 | tf_op jit(solution)/shard_map/psum | solution.py:106
  979.2 123.1 %all-reduce.27.cloned.1.call-done = (f32[4096]{0:T(1024)}, f32[4096]{0:T(1024)}, f32[4096]{0:T(1024)}, f32[4096]{0:T(1024)}, f32[4096]{0:T(1024)}, /*index=5*/f32[4096]{0:T(1024)}) async-done(((f32[4096]{0:T(1024)}, f32[4096]{0:T(1024)}, f32[4096]{0:T(1024)}, f32[4096]{0:T(1024)}, f32[4096]{0:T(1024)}, /*index=5*/f32[4096]{0:T(1024)}), (f32[4096]{0:T(1024)}, f32[4096]{0:T(1024)}, f32[4096]{0:T(1024)}, ...) | async-done | bytes 98320 | tf_op jit(solution)/shard_map/psum | solution.py:106
  1117.5 41.6 %all-reduce.10 = (f32[512]{0:T(512)S(1)}, f32[512]{0:T(512)S(1)}, f32[512]{0:T(512)S(1)}, f32[512]{0:T(512)S(1)}, f32[512]{0:T(512)S(1)}, /*index=5*/f32[512]{0:T(512)S(1)}) all-reduce(f32[512]{0:T(512)S(1)} %get-tuple-element.485, f32[512]{0:T(512)S(1)} %get-tuple-element.484, ...), channel_id=1, replica_groups=mesh['dp'=8,'rep'=4] {'dp','rep'}, use_global_device_ids=true, to_apply=%region_93.94 | all-reduce | flops 3072 | bytes 24576 | tf_op jit(solution)/shard_map/psum | solution.py:106
  1247.0 8.8 scatter_fusion.20
  1255.7 8.8 scatter_fusion.21
  1264.5 8.8 scatter_fusion.22
  1273.3 8.8 scatter_fusion.23
  1282.1 5.4 scatter_fusion.24
  1287.5 5.4 scatter_fusion.25
  1292.8 5.4 scatter_fusion.26
  1298.2 5.6 scatter_fusion.27
  1303.9 8.8 scatter_fusion.28
  1315.7 39.9 %all-reduce.9 = (f32[512]{0:T(512)S(1)}, f32[512]{0:T(512)S(1)}, f32[512]{0:T(512)S(1)}, f32[512]{0:T(512)S(1)}, f32[512]{0:T(512)S(1)}, /*index=5*/f32[512]{0:T(512)S(1)}) all-reduce(f32[512]{0:T(512)S(1)} %copy-done.285, f32[512]{0:T(512)S(1)} %copy-done.284, ...), channel_id=1, replica_groups=mesh['dp'=8,'rep'=4] {'dp','rep'}, use_global_device_ids=true, to_apply=%region_106.107 | all-reduce | flops 3072 | bytes 24576 | tf_op jit(solution)/shard_map/psum | solution.py:106
  1394.8 5.9 bitcast_add_fusion.4
  1403.7 5.3 fusion.84
  1408.9 7.6 bitcast_add_fusion
  1416.5 9.7 copy.320
  1430.1 6.8 fusion.86
  1436.9 8.5 bitcast_add_fusion.2
  1445.4 9.6 copy.295
  1461.7 5.2 stack.136
  1489.1 7.4 scatter_fusion.19
  1502.8 22.2 reduce-scatter.16.cloned.1.call-done
  1526.8 90.4 %reduce-scatter.20.cloned.1.call-done = f32[512,256]{1,0:T(8,128)} async-done(((f32[512,2048]{1,0:T(8,128)}), f32[512,256]{1,0:T(8,128)}) %reduce-scatter.20.cloned.1.call-update) | async-done | bytes 524304 | tf_op jit(solution)/shard_map/reduce_scatter | solution.py:298
  1619.0 90.1 %reduce-scatter.12.cloned.1.call-done = f32[512,256]{1,0:T(8,128)} async-done(((f32[512,2048]{1,0:T(8,128)}), f32[512,256]{1,0:T(8,128)}) %reduce-scatter.12.cloned.1.call-update) | async-done | bytes 524304 | tf_op jit(solution)/shard_map/reduce_scatter | solution.py:364
  1710.8 151.4 %reduce-scatter.14.cloned.1.call-done = f32[1024,256]{1,0:T(8,128)} async-done(((f32[1024,2048]{1,0:T(8,128)}), f32[1024,256]{1,0:T(8,128)}) %reduce-scatter.14.cloned.1.call-update) | async-done | bytes 1048592 | tf_op jit(solution)/shard_map/reduce_scatter | solution.py:365
  1864.3 164.1 %reduce-scatter.18.cloned.1.call-done = f32[3,3,512,64]{2,3,1,0:T(8,128)} async-done(((f32[3,3,512,512]{2,3,1,0:T(8,128)}), f32[3,3,512,64]{2,3,1,0:T(8,128)}) %reduce-scatter.18.cloned.1.call-update) | async-done | bytes 1179664 | tf_op jit(solution)/shard_map/reduce_scatter | solution.py:297
  2030.6 164.1 %reduce-scatter.10.cloned.1.call-done = f32[3,3,512,64]{2,3,1,0:T(8,128)} async-done(((f32[3,3,512,512]{2,3,1,0:T(8,128)}), f32[3,3,512,64]{2,3,1,0:T(8,128)}) %reduce-scatter.10.cloned.1.call-update) | async-done | bytes 1179664 | tf_op jit(solution)/shard_map/reduce_scatter | solution.py:363
  2202.2 11.2 scatter_fusion.29
  2216.6 43.2 %all-reduce.31.cloned.1.call-done = (bf16[1024,64]{0,1:T(8,128)(2,1)}, bf16[3,3,512,64]{2,3,1,0:T(8,128)(2,1)}, bf16[512,256]{1,0:T(8,128)(2,1)}, bf16[1024,256]...) async-done(((bf16[1024,64]{0,1:T(8,128)(2,1)}, bf16[3,3,512,64]{2,3,1,0:T(8,128)(2,1)}, ...) | async-done | bytes 2621456 | tf_op jit(solution)/shard_map/psum | solution.py:368
  2279.7 21.5 all-reduce.21
  (1169 shorter events, 581.5 us)
Async XLA Ops:
  7.2 61.0 %all-gather.12.cloned.1.call-start = ((), (), s32[]{:S(2)}) async-start(), calls=%async_computation.7 | async-start | bytes 1179648 | tf_op jit(solution)/shard_map/all_gather | solution.py:175
  8.0 254.8 %all-gather.18.cloned.1.call-start = ((), (), s32[]{:S(2)}) async-start(), calls=%async_computation.10 | async-start | bytes 4718592 | tf_op jit(solution)/shard_map/all_gather | solution.py:181
  8.7 262.2 %all-gather.14.cloned.1.call-start = ((), (), s32[]{:S(2)}) async-start(), calls=%async_computation.8 | async-start | bytes 5308416 | tf_op jit(solution)/shard_map/all_gather | solution.py:177
  9.5 29.3 %copy-start.310 = (bf16[2,64]{1,0:T(2,128)(2,1)S(1)}, bf16[2,64]{1,0:T(2,128)(2,1)}, u32[]{:S(2)}) copy-start(bf16[2,64]{1,0:T(2,128)(2,1)} %param.85) | copy-start | bytes 772
  9.5 46.2 %copy-start.71 = (bf16[2,14,14,1024]{3,0,2,1:T(2,128)(2,1)S(1)}, bf16[2,14,14,1024]{3,0,2,1:T(2,128)(2,1)}, u32[]{:S(2)}) copy-start(bf16[2,14,14,1024]{3,0,2,1:T(2,128)(2,1)} %param.76) | copy-start | bytes 2408452
  9.5 324.7 %all-gather.16.cloned.1.call-start = ((), (), s32[]{:S(2)}) async-start(), calls=%async_computation.9 | async-start | bytes 2359296 | tf_op jit(solution)/shard_map/all_gather | solution.py:179
  10.1 435.1 %all-gather.22.cloned.1.call-start = ((), (), s32[]{:S(2)}) async-start(), calls=%async_computation.12 | async-start | bytes 5308416 | tf_op jit(solution)/shard_map/all_gather | solution.py:221
  10.6 460.4 %all-reduce.29.cloned.1.call-start = ((), (), s32[]{:S(2)}) async-start(), calls=%async_computation.22 | async-start | bytes 196608 | tf_op jit(solution)/shard_map/psum | solution.py:75
  11.9 614.1 %copy-start.187 = (f32[4]{0:T(128)}, f32[4]{0:T(128)S(1)}, u32[]{:S(2)}) copy-start(f32[4]{0:T(128)S(1)} %compare_convert_fusion.2) | copy-start | bytes 52
  12.6 55.7 %copy-start.307 = (bf16[4]{0:T(256)(128)(2,1)}, bf16[4]{0:T(256)(128)(2,1)S(1)}, u32[]{:S(2)}) copy-start(bf16[4]{0:T(256)(128)(2,1)S(1)} %fusion.254) | copy-start | bytes 28
  13.9 56.9 %copy-start.296 = (bf16[2]{0:T(256)(128)(2,1)}, bf16[2]{0:T(256)(128)(2,1)S(1)}, u32[]{:S(2)}) copy-start(bf16[2]{0:T(256)(128)(2,1)S(1)} %fusion.255) | copy-start | bytes 16
  14.6 328.3 %copy-start.213 = (f32[2]{0:T(128)}, f32[2]{0:T(128)S(1)}, u32[]{:S(2)}) copy-start(f32[2]{0:T(128)S(1)} %compare_convert_fusion) | copy-start | bytes 28
  16.5 250.6 %copy-start.117 = (bf16[4,5,5,1024]{3,2,1,0:T(8,128)(2,1)}, bf16[4,5,5,1024]{3,2,1,0:T(8,128)(2,1)S(1)}, u32[]{:S(2)}) copy-start(bf16[4,5,5,1024]{3,2,1,0:T(8,128)(2,1)S(1)} %slice.1455) | copy-start | bytes 614404
  55.6 286.3 %copy-start.200 = (f32[1,512]{1,0:T(1,128)}, f32[1,512]{1,0:T(1,128)S(1)}, u32[]{:S(2)}) copy-start(f32[1,512]{1,0:T(1,128)S(1)} %get-tuple-element.750) | copy-start | bytes 6148
  70.8 51.1 %copy-start.27 = (f32[4,10,10,512]{3,2,1,0:T(8,128)}, f32[4,10,10,512]{3,2,1,0:T(8,128)S(1)}, u32[]{:S(2)}) copy-start(f32[4,10,10,512]{3,2,1,0:T(8,128)S(1)} %get-tuple-element.810) | copy-start | bytes 2457604
  74.0 49.1 %copy-start.25 = (f32[2,18,18,512]{3,2,1,0:T(8,128)}, f32[2,18,18,512]{3,2,1,0:T(8,128)S(1)}, u32[]{:S(2)}) copy-start(f32[2,18,18,512]{3,2,1,0:T(8,128)S(1)} %get-tuple-element.812) | copy-start | bytes 3981316
  231.4 20.2 copy-start.146
  231.4 20.9 copy-start.145
  233.4 19.6 copy-start.144
  236.5 17.1 copy-start.143
  281.7 52.5 %copy-start.102 = (f32[2,7,7,512]{3,2,1,0:T(8,128)}, f32[2,7,7,512]{3,2,1,0:T(8,128)S(1)}, u32[]{:S(2)}) copy-start(f32[2,7,7,512]{3,2,1,0:T(8,128)S(1)} %get-tuple-element.814) | copy-start | bytes 602116
  284.9 54.4 %copy-start.112 = (f32[4,5,5,512]{3,2,1,0:T(8,128)}, f32[4,5,5,512]{3,2,1,0:T(8,128)S(1)}, u32[]{:S(2)}) copy-start(f32[4,5,5,512]{3,2,1,0:T(8,128)S(1)} %get-tuple-element.813) | copy-start | bytes 614404
  284.9 49.3 %copy-start.237 = (f32[1,512]{1,0:T(1,128)S(1)}, f32[1,512]{1,0:T(1,128)}, u32[]{:S(2)}) copy-start(f32[1,512]{1,0:T(1,128)} %get-tuple-element.751) | copy-start | bytes 6148
  334.1 291.2 %copy-start.198 = (f32[512]{0:T(512)}, f32[512]{0:T(512)S(1)}, u32[]{:S(2)}) copy-start(f32[512]{0:T(512)S(1)} %get-tuple-element.743) | copy-start | bytes 6148
  339.2 285.4 %copy-start.240 = (f32[512]{0:T(512)}, f32[512]{0:T(512)S(1)}, u32[]{:S(2)}) copy-start(f32[512]{0:T(512)S(1)} %get-tuple-element.745) | copy-start | bytes 6148
  341.9 283.4 %copy-start.243 = (f32[512]{0:T(512)}, f32[512]{0:T(512)S(1)}, u32[]{:S(2)}) copy-start(f32[512]{0:T(512)S(1)} %get-tuple-element.741) | copy-start | bytes 6148
  343.0 28.1 %copy-start.305 = (bf16[2,256]{1,0:T(2,128)(2,1)S(1)}, bf16[2,256]{1,0:T(2,128)(2,1)}, u32[]{:S(2)}) copy-start(bf16[2,256]{1,0:T(2,128)(2,1)} %param.89) | copy-start | bytes 3076
  343.0 44.4 %copy-start.311 = (bf16[2,64]{1,0:T(2,128)(2,1)S(1)}, bf16[2,64]{1,0:T(2,128)(2,1)}, u32[]{:S(2)}) copy-start(bf16[2,64]{1,0:T(2,128)(2,1)} %param.91) | copy-start | bytes 772
  343.0 62.6 %copy-start.312 = (bf16[2,64]{1,0:T(2,128)(2,1)S(1)}, bf16[2,64]{1,0:T(2,128)(2,1)}, u32[]{:S(2)}) copy-start(bf16[2,64]{1,0:T(2,128)(2,1)} %param.93) | copy-start | bytes 772
  343.0 79.5 %copy-start.306 = (bf16[2,256]{1,0:T(2,128)(2,1)S(1)}, bf16[2,256]{1,0:T(2,128)(2,1)}, u32[]{:S(2)}) copy-start(bf16[2,256]{1,0:T(2,128)(2,1)} %param.95) | copy-start | bytes 3076
  343.0 101.4 %copy-start.319 = (s32[4]{0:T(128)S(1)}, s32[4]{0:T(128)}, u32[]{:S(2)}) copy-start(s32[4]{0:T(128)} %constant.735.clone.1) | copy-start | bytes 52
  344.6 178.9 %all-gather.20.cloned.1.call-start = ((), (), s32[]{:S(2)}) async-start(), calls=%async_computation.11 | async-start | bytes 2359296 | tf_op jit(solution)/shard_map/all_gather | solution.py:219
  345.4 280.7 %all-gather.24.cloned.1.call-start = ((), (), s32[]{:S(2)}) async-start(), calls=%async_computation.13 | async-start | bytes 2359296 | tf_op jit(solution)/shard_map/all_gather | solution.py:223
  346.1 756.2 %all-reduce.27.cloned.1.call-start = ((), (), s32[]{:S(2)}) async-start(), calls=%async_computation.21 | async-start | bytes 196608 | tf_op jit(solution)/shard_map/psum | solution.py:106
  422.5 209.1 %copy-start.254 = (f32[1,512]{1,0:T(1,128)}, f32[1,512]{1,0:T(1,128)S(1)}, u32[]{:S(2)}) copy-start(f32[1,512]{1,0:T(1,128)S(1)} %get-tuple-element.734) | copy-start | bytes 6148
  471.8 496.7 %copy-start.172 = (f32[4096]{0:T(1024)}, f32[4096]{0:T(1024)S(1)}, u32[]{:S(2)}) copy-start(f32[4096]{0:T(1024)S(1)} %get-tuple-element.662) | copy-start | bytes 49156
  477.3 49.8 %copy-start.67 = (bf16[2,7,7,2048]{3,2,1,0:T(8,128)(2,1)}, bf16[2,7,7,2048]{3,2,1,0:T(8,128)(2,1)S(1)}, u32[]{:S(2)}) copy-start(bf16[2,7,7,2048]{3,2,1,0:T(8,128)(2,1)S(1)} %multiply_convert_fusion.13) | copy-start | bytes 1204228
  528.4 47.4 %slice-start = ((s8[4718592]{0:T(1024)(128)(4,1)}), s8[524288]{0:T(1024)(128)(4,1)S(1)}, s32[]{:S(2)}) async-start(s8[4718592]{0:T(1024)(128)(4,1)} %bitcast.521), calls=%async_computation.24 | async-start | bytes 1048576
  573.4 284.0 %copy-start.183 = (f32[512]{0:T(512)}, f32[512]{0:T(512)S(1)}, u32[]{:S(2)}) copy-start(f32[512]{0:T(512)S(1)} %get-tuple-element.733) | copy-start | bytes 6148
  574.4 51.0 %copy-start.185 = (f32[512]{0:T(512)}, f32[512]{0:T(512)S(1)}, u32[]{:S(2)}) copy-start(f32[512]{0:T(512)S(1)} %get-tuple-element.731) | copy-start | bytes 6148
  580.8 43.8 %copy-start.201 = (f32[1,512]{1,0:T(1,128)S(1)}, f32[1,512]{1,0:T(1,128)}, u32[]{:S(2)}) copy-start(f32[1,512]{1,0:T(1,128)} %copy-done.200) | copy-start | bytes 6148
  580.8 43.8 %copy-start.211 = (f32[512]{0:T(512)S(1)}, f32[512]{0:T(512)}, u32[]{:S(2)}) copy-start(f32[512]{0:T(512)} %copy-done.210) | copy-start | bytes 6148
  580.8 44.5 %copy-start.192 = (f32[512]{0:T(512)S(1)}, f32[512]{0:T(512)}, u32[]{:S(2)}) copy-start(f32[512]{0:T(512)} %copy-done.191) | copy-start | bytes 6148
  580.8 44.5 %copy-start.208 = (f32[512]{0:T(512)S(1)}, f32[512]{0:T(512)}, u32[]{:S(2)}) copy-start(f32[512]{0:T(512)} %copy-done.207) | copy-start | bytes 6148
  580.8 45.2 %copy-start.299 = (f32[1,512]{1,0:T(1,128)S(1)}, f32[1,512]{1,0:T(1,128)}, u32[]{:S(2)}) copy-start(f32[1,512]{1,0:T(1,128)} %get-tuple-element.735) | copy-start | bytes 6148
  624.5 157.3 %copy-start.249 = (f32[512]{0:T(512)}, f32[512]{0:T(512)S(1)}, u32[]{:S(2)}) copy-start(f32[512]{0:T(512)S(1)} %get-tuple-element.729) | copy-start | bytes 6148
  624.6 112.9 %copy-start.246 = (f32[512]{0:T(512)}, f32[512]{0:T(512)S(1)}, u32[]{:S(2)}) copy-start(f32[512]{0:T(512)S(1)} %get-tuple-element.727) | copy-start | bytes 6148
  631.6 42.4 %copy-start.188 = (f32[4]{0:T(128)S(1)}, f32[4]{0:T(128)}, u32[]{:S(2)}) copy-start(f32[4]{0:T(128)} %copy-done.187) | copy-start | bytes 52
  631.7 42.5 %copy-start.215 = (f32[2]{0:T(128)S(1)}, f32[2]{0:T(128)}, u32[]{:S(2)}) copy-start(f32[2]{0:T(128)} %copy-done.213) | copy-start | bytes 28
  631.7 51.3 %slice-start.4 = ((s8[4718592]{0:T(1024)(128)(4,1)}), s8[524288]{0:T(1024)(128)(4,1)S(1)}, s32[]{:S(2)}) async-start(s8[4718592]{0:T(1024)(128)(4,1)} %bitcast.530), calls=%async_computation.28 | async-start | bytes 1048576
  913.7 49.8 %copy-start.56 = (f32[4,5,5,512]{3,2,1,0:T(8,128)S(1)}, f32[4,5,5,512]{3,2,1,0:T(8,128)}, u32[]{:S(2)}) copy-start(f32[4,5,5,512]{3,2,1,0:T(8,128)} %get-tuple-element.816) | copy-start | bytes 614404
  913.7 49.8 %copy-start.226 = (f32[4,512]{1,0:T(4,128)S(1)}, f32[4,512]{1,0:T(4,128)}, u32[]{:S(2)}) copy-start(f32[4,512]{1,0:T(4,128)} %get-tuple-element.798) | copy-start | bytes 24580
  977.0 128.0 %copy-start.173 = (f32[4096]{0:T(1024)S(1)}, f32[4096]{0:T(1024)}, u32[]{:S(2)}) copy-start(f32[4096]{0:T(1024)} %copy-done.172) | copy-start | bytes 49156
  979.1 522.1 %reduce-scatter.8.cloned.1.call-start = ((), (), s32[]{:S(2)}) async-start(), calls=%async_computation.14 | async-start | bytes 2359296 | tf_op jit(solution)/shard_map/reduce_scatter | solution.py:362
  1115.6 44.7 %copy-start.225 = (f32[4,512]{1,0:T(4,128)S(1)}, f32[4,512]{1,0:T(4,128)}, u32[]{:S(2)}) copy-start(f32[4,512]{1,0:T(4,128)} %get-tuple-element.799) | copy-start | bytes 24580
  1313.3 43.5 %copy-start.258 = (f32[2,512]{1,0:T(2,128)S(1)}, f32[2,512]{1,0:T(2,128)}, u32[]{:S(2)}) copy-start(f32[2,512]{1,0:T(2,128)} %get-tuple-element.757) | copy-start | bytes 12292
  1366.6 158.5 %reduce-scatter.16.cloned.1.call-start = ((), (), s32[]{:S(2)}) async-start(), calls=%async_computation.18 | async-start | bytes 4718592 | tf_op jit(solution)/shard_map/reduce_scatter | solution.py:296
  1373.2 244.0 %reduce-scatter.20.cloned.1.call-start = ((), (), s32[]{:S(2)}) async-start(), calls=%async_computation.20 | async-start | bytes 4718592 | tf_op jit(solution)/shard_map/reduce_scatter | solution.py:298
  1380.2 328.9 %reduce-scatter.12.cloned.1.call-start = ((), (), s32[]{:S(2)}) async-start(), calls=%async_computation.16 | async-start | bytes 4718592 | tf_op jit(solution)/shard_map/reduce_scatter | solution.py:364
  1390.9 471.3 %reduce-scatter.14.cloned.1.call-start = ((), (), s32[]{:S(2)}) async-start(), calls=%async_computation.17 | async-start | bytes 9437184 | tf_op jit(solution)/shard_map/reduce_scatter | solution.py:365
  1400.7 627.6 %reduce-scatter.18.cloned.1.call-start = ((), (), s32[]{:S(2)}) async-start(), calls=%async_computation.19 | async-start | bytes 10616832 | tf_op jit(solution)/shard_map/reduce_scatter | solution.py:297
  1426.3 768.4 %reduce-scatter.10.cloned.1.call-start = ((), (), s32[]{:S(2)}) async-start(), calls=%async_computation.15 | async-start | bytes 10616832 | tf_op jit(solution)/shard_map/reduce_scatter | solution.py:363
  1455.1 804.6 %all-reduce.31.cloned.1.call-start = ((), (), s32[]{:S(2)}) async-start(), calls=%async_computation.23 | async-start | bytes 5242880 | tf_op jit(solution)/shard_map/psum | solution.py:368
  2279.7 27.8 %copy-start.97 = (f32[512,256]{1,0:T(8,128)S(1)}, f32[512,256]{1,0:T(8,128)}, u32[]{:S(2)}) copy-start(f32[512,256]{1,0:T(8,128)} %get-tuple-element.599) | copy-start | bytes 1572868
  (284 other events, 977.7 us)
Sparse Core Ops, SparseCore 0:
  10.2 42.9 all-gather.11
  55.2 73.8 all-gather.17
  131.3 78.1 all-gather.13
  211.4 49.2 all-gather.15
  262.7 78.6 all-gather.21
  349.4 121.6 all-reduce.28
  473.2 50.3 all-gather.19
  525.6 50.9 all-gather.23
  979.2 123.0 all-reduce.26
  1366.7 67.6 reduce-scatter.7
  1438.0 87.0 reduce-scatter.15
  1529.0 88.1 reduce-scatter.19
  1620.8 88.1 reduce-scatter.11
  1713.0 149.1 reduce-scatter.13
  1865.6 162.6 reduce-scatter.17
  2031.8 162.7 reduce-scatter.9
  2199.6 60.0 all-reduce.30
where the time goes:
time: 2340 us; the launch traced here: 2320 us
  waiting for transfers between devices  912 us (39%)
  blocking collectives  565 us (24%)
  other arithmetic  335 us (14%)
  local copies, waits for them, and re-layouts  331 us (14%)
  matrix products  157 us (7%)
    psum x5, blocking collectives, batch_norm(): lax.psum((firsts[0], seconds[0], firsts[1], seconds[1], firsts[2], second...  212 us
    psum x5, blocking collectives, norm_back(): lax.psum((firsts[0], seconds[0], firsts[1], seconds[1], firsts[2], second...  204 us
    reduce_scatter x1, waiting for transfers between devices, on_device(): lax.psum_scatter(term_b2, 'dp', scatter_dimension=3, tiled=True)  164 us
    reduce_scatter x1, waiting for transfers between devices, on_device(): lax.psum_scatter(term_a2, 'dp', scatter_dimension=3, tiled=True)  164 us
    reduce_scatter x1, waiting for transfers between devices, on_device(): lax.psum_scatter(term_as, 'dp', scatter_dimension=1, tiled=True)  151 us
    psum x1, waiting for transfers between devices, norm_back(): lax.psum((firsts[0], seconds[0], firsts[1], seconds[1], firsts[2], second...  123 us
    scatter-add x27, other arithmetic, fold_patches(): padded = padded.at[:, offset_row:offset_row + side_in:stride, offset_col:...  122 us
    slice x27, local copies, waits for them, and re-layouts, patches(): padded[:, offset_row:offset_row + extent:stride, offset_col:offset_col +...  107 us
  transfers between devices with their start and end apart: 17, of which 10 were waited for; matrix products, arithmetic and copies ran while one was open for 17% of the time, Pallas kernels for 0%

commit v1 on v0

--- a/solution.py
+++ b/solution.py
@@ -1,8 +1,14 @@
+import functools
+
 import jax
 import jax.numpy as jnp
+import numpy as np
 from jax import lax
+from jax.experimental import pallas as pl
+from jax.experimental.pallas import tpu as pltpu
 from jax.sharding import PartitionSpec as P
 
+DP, REP = "dp", "rep"
 EPSILON = 1e-05
 DECAY_RATE = 5e-05
 
@@ -13,15 +19,15 @@
 
 
 def pointwise(inputs, weight):
-    return jnp.einsum("nhwc,cd->nhwd", inputs, weight, preferred_element_type=jnp.float32)
+    return jnp.tensordot(inputs, weight, 1, preferred_element_type=jnp.float32)
 
 
 def pointwise_back(upstream, weight):
-    return jnp.einsum("nhwd,cd->nhwc", upstream, weight, preferred_element_type=jnp.float32)
+    return jnp.tensordot(upstream, weight, ((3,), (1,)), preferred_element_type=jnp.float32)
 
 
 def weight_term(inputs, upstream):
-    return jnp.einsum("nhwc,nhwd->cd", inputs, upstream, preferred_element_type=jnp.float32)
+    return jnp.tensordot(inputs, upstream, ((0, 1, 2),) * 2, preferred_element_type=jnp.float32)
 
 
 def summed_terms(inputs, upstream):
@@ -73,7 +79,7 @@
         firsts.append(jnp.sum(weighted, axis=(0, 1, 2)))
         seconds.append(jnp.sum(weighted * values[group_member], axis=(0, 1, 2)))
     summed = lax.psum(
-        (firsts[0], seconds[0], firsts[1], seconds[1], firsts[2], seconds[2]), ("dp", "rep")
+        (firsts[0], seconds[0], firsts[1], seconds[1], firsts[2], seconds[2]), (DP, REP)
     )
     normed = []
     means = []
@@ -104,7 +110,7 @@
         firsts.append(jnp.sum(weighted, axis=(0, 1, 2)))
         seconds.append(jnp.sum(weighted * normal, axis=(0, 1, 2)))
     summed = lax.psum(
-        (firsts[0], seconds[0], firsts[1], seconds[1], firsts[2], seconds[2]), ("dp", "rep")
+        (firsts[0], seconds[0], firsts[1], seconds[1], firsts[2], seconds[2]), (DP, REP)
     )
     results = []
     for group_member in range(3):
@@ -126,10 +132,10 @@
 
 
 def own_columns(full, local_width):
-    return lax.dynamic_slice_in_dim(full, lax.axis_index("dp") * local_width, local_width, 1)
-
-
-def on_device(
+    return lax.dynamic_slice_in_dim(full, lax.axis_index(DP) * local_width, local_width, 1)
+
+
+def plain_on_device(
     input_160,
     input_224,
     input_288,
@@ -165,21 +171,21 @@
         )
         live_masks.append(live_flags)
         masked.append(inputs[group_member] * live_flags.astype(jnp.bfloat16))
-    totals = lax.psum(live_counts[0].astype(jnp.float32), ("dp", "rep"))
+    totals = lax.psum(live_counts[0].astype(jnp.float32), (DP, REP))
     local_weights = (conv_a1, conv_a2, conv_a3, conv_as, conv_b1, conv_b2, conv_b3)
     squares_list = []
     for weight in local_weights:
         squares_list.append(jnp.sum(jnp.square(weight.astype(jnp.float32))))
     weight_squares = jnp.stack(squares_list)
     gathered_a = (
-        lax.all_gather(conv_a1, "dp", axis=1, tiled=True),
-        lax.all_gather(norm_a1, "dp", axis=1, tiled=True),
-        lax.all_gather(conv_a2, "dp", axis=3, tiled=True),
-        lax.all_gather(norm_a2, "dp", axis=1, tiled=True),
-        lax.all_gather(conv_a3, "dp", axis=1, tiled=True),
-        lax.all_gather(norm_a3, "dp", axis=1, tiled=True),
-        lax.all_gather(conv_as, "dp", axis=1, tiled=True),
-        lax.all_gather(norm_as, "dp", axis=1, tiled=True),
+        lax.all_gather(conv_a1, DP, axis=1, tiled=True),
+        lax.all_gather(norm_a1, DP, axis=1, tiled=True),
+        lax.all_gather(conv_a2, DP, axis=3, tiled=True),
+        lax.all_gather(norm_a2, DP, axis=1, tiled=True),
+        lax.all_gather(conv_a3, DP, axis=1, tiled=True),
+        lax.all_gather(norm_a3, DP, axis=1, tiled=True),
+        lax.all_gather(conv_as, DP, axis=1, tiled=True),
+        lax.all_gather(norm_as, DP, axis=1, tiled=True),
     )
     full_a1, param_a1, full_a2, param_a2, full_a3, param_a3, full_as, param_as = gathered_a
     mid_width = full_a2.shape[3]
@@ -216,12 +222,12 @@
         for group_member in range(3)
     ]
     gathered_b = (
-        lax.all_gather(conv_b1, "dp", axis=1, tiled=True),
-        lax.all_gather(norm_b1, "dp", axis=1, tiled=True),
-        lax.all_gather(conv_b2, "dp", axis=3, tiled=True),
-        lax.all_gather(norm_b2, "dp", axis=1, tiled=True),
-        lax.all_gather(conv_b3, "dp", axis=1, tiled=True),
-        lax.all_gather(norm_b3, "dp", axis=1, tiled=True),
+        lax.all_gather(conv_b1, DP, axis=1, tiled=True),
+        lax.all_gather(norm_b1, DP, axis=1, tiled=True),
+        lax.all_gather(conv_b2, DP, axis=3, tiled=True),
+        lax.all_gather(norm_b2, DP, axis=1, tiled=True),
+        lax.all_gather(conv_b3, DP, axis=1, tiled=True),
+        lax.all_gather(norm_b3, DP, axis=1, tiled=True),
     )
     full_b1, param_b1, full_b2, param_b2, full_b3, param_b3 = gathered_b
     hidden_b1 = [pointwise(out_a[group_member], full_b1) for group_member in range(3)]
@@ -248,12 +254,12 @@
         for group_member in range(3)
     ]
     back_b = (
-        lax.all_gather(conv_b1, "dp", axis=1, tiled=True),
-        lax.all_gather(norm_b1, "dp", axis=1, tiled=True),
-        lax.all_gather(conv_b2, "dp", axis=3, tiled=True),
-        lax.all_gather(norm_b2, "dp", axis=1, tiled=True),
-        lax.all_gather(conv_b3, "dp", axis=1, tiled=True),
-        lax.all_gather(norm_b3, "dp", axis=1, tiled=True),
+        lax.all_gather(conv_b1, DP, axis=1, tiled=True),
+        lax.all_gather(norm_b1, DP, axis=1, tiled=True),
+        lax.all_gather(conv_b2, DP, axis=3, tiled=True),
+        lax.all_gather(norm_b2, DP, axis=1, tiled=True),
+        lax.all_gather(conv_b3, DP, axis=1, tiled=True),
+        lax.all_gather(norm_b3, DP, axis=1, tiled=True),
     )
     full_b1, param_b1, full_b2, param_b2, full_b3, param_b3 = back_b
     kernel_b2 = full_b2.reshape(9 * mid_width, mid_width)
@@ -293,24 +299,24 @@
         for group_member in range(3)
     ]
     shard_b = (
-        lax.psum_scatter(term_b1, "dp", scatter_dimension=1, tiled=True),
-        lax.psum_scatter(term_b2, "dp", scatter_dimension=3, tiled=True),
-        lax.psum_scatter(term_b3, "dp", scatter_dimension=1, tiled=True),
+        lax.psum_scatter(term_b1, DP, scatter_dimension=1, tiled=True),
+        lax.psum_scatter(term_b2, DP, scatter_dimension=3, tiled=True),
+        lax.psum_scatter(term_b3, DP, scatter_dimension=1, tiled=True),
     )
     grads_b = (
-        lax.psum(shard_b[0].astype(jnp.bfloat16), "rep").astype(jnp.float32),
-        lax.psum(shard_b[1].astype(jnp.bfloat16), "rep").astype(jnp.float32),
-        lax.psum(shard_b[2].astype(jnp.bfloat16), "rep").astype(jnp.float32),
+        lax.psum(shard_b[0].astype(jnp.bfloat16), REP).astype(jnp.float32),
+        lax.psum(shard_b[1].astype(jnp.bfloat16), REP).astype(jnp.float32),
+        lax.psum(shard_b[2].astype(jnp.bfloat16), REP).astype(jnp.float32),
     )
     back_a = (
-        lax.all_gather(conv_a1, "dp", axis=1, tiled=True),
-        lax.all_gather(norm_a1, "dp", axis=1, tiled=True),
-        lax.all_gather(conv_a2, "dp", axis=3, tiled=True),
-        lax.all_gather(norm_a2, "dp", axis=1, tiled=True),
-        lax.all_gather(conv_a3, "dp", axis=1, tiled=True),
-        lax.all_gather(norm_a3, "dp", axis=1, tiled=True),
-        lax.all_gather(conv_as, "dp", axis=1, tiled=True),
-        lax.all_gather(norm_as, "dp", axis=1, tiled=True),
+        lax.all_gather(conv_a1, DP, axis=1, tiled=True),
+        lax.all_gather(norm_a1, DP, axis=1, tiled=True),
+        lax.all_gather(conv_a2, DP, axis=3, tiled=True),
+        lax.all_gather(norm_a2, DP, axis=1, tiled=True),
+        lax.all_gather(conv_a3, DP, axis=1, tiled=True),
+        lax.all_gather(norm_a3, DP, axis=1, tiled=True),
+        lax.all_gather(conv_as, DP, axis=1, tiled=True),
+        lax.all_gather(norm_as, DP, axis=1, tiled=True),
     )
     full_a1, param_a1, full_a2, param_a2, full_a3, param_a3, full_as, param_as = back_a
     kernel_a2 = full_a2.reshape(9 * mid_width, mid_width)
@@ -359,16 +365,16 @@
         for group_member in range(3)
     ]
     shard_a = (
-        lax.psum_scatter(term_a1, "dp", scatter_dimension=1, tiled=True),
-        lax.psum_scatter(term_a2, "dp", scatter_dimension=3, tiled=True),
-        lax.psum_scatter(term_a3, "dp", scatter_dimension=1, tiled=True),
-        lax.psum_scatter(term_as, "dp", scatter_dimension=1, tiled=True),
+        lax.psum_scatter(term_a1, DP, scatter_dimension=1, tiled=True),
+        lax.psum_scatter(term_a2, DP, scatter_dimension=3, tiled=True),
+        lax.psum_scatter(term_a3, DP, scatter_dimension=1, tiled=True),
+        lax.psum_scatter(term_as, DP, scatter_dimension=1, tiled=True),
     )
     grads_a = (
-        lax.psum(shard_a[0].astype(jnp.bfloat16), "rep").astype(jnp.float32),
-        lax.psum(shard_a[1].astype(jnp.bfloat16), "rep").astype(jnp.float32),
-        lax.psum(shard_a[2].astype(jnp.bfloat16), "rep").astype(jnp.float32),
-        lax.psum(shard_a[3].astype(jnp.bfloat16), "rep").astype(jnp.float32),
+        lax.psum(shard_a[0].astype(jnp.bfloat16), REP).astype(jnp.float32),
+        lax.psum(shard_a[1].astype(jnp.bfloat16), REP).astype(jnp.float32),
+        lax.psum(shard_a[2].astype(jnp.bfloat16), REP).astype(jnp.float32),
+        lax.psum(shard_a[3].astype(jnp.bfloat16), REP).astype(jnp.float32),
     )
     mid_local = norm_a1.shape[1]
     out_local = norm_a3.shape[1]
@@ -384,7 +390,7 @@
     for gradient in gradients:
         grad_list.append(jnp.sum(gradient * gradient))
     grad_squares = jnp.stack(grad_list)
-    weight_totals, grad_totals = lax.psum((weight_squares, grad_squares), "dp")
+    weight_totals, grad_totals = lax.psum((weight_squares, grad_squares), DP)
     weight_norm = jnp.sqrt(weight_totals)
     grad_norm = jnp.sqrt(grad_totals)
     trust_ratio = weight_norm / (grad_norm + DECAY_RATE * weight_norm)
@@ -425,63 +431,1703 @@
     )
 
 
+MESH = pl.DeviceIdType.MESH
+ANY = pl.BlockSpec(memory_space=pl.ANY)
+
+
+def position():
+    dp, rep = lax.axis_index(DP), lax.axis_index(REP)
+    return dp // 2, lax.rem(dp, 2), rep // 2, lax.rem(rep, 2)
+
+
+def device_at(z, x, y, core):
+    return (z * 2 + x, y * 2 + core)
+
+
+def greet(depth):
+    z, x, y, core = position()
+    barrier = pltpu.get_barrier_semaphore()
+    peers = [(z, x, y, 1 - core), (z, x, 1 - y, core), (z, x, 1 - y, 1 - core)]
+    peers += [(z, 1 - x, y, core), (z, 1 - x, y, 1 - core), (z, 1 - x, 1 - y, core), (z, 1 - x, 1 - y, 1 - core)]
+    peers += [(lax.rem(z + step, depth), x, y, core) for step in range(1, depth)]
+    for peer in peers:
+        pl.semaphore_signal(barrier, inc=1, device_id=device_at(*peer), device_id_type=MESH)
+    pl.semaphore_wait(barrier, len(peers))
+
+
+def remote(src, dst, send, recv, peer):
+    return pltpu.make_async_remote_copy(
+        src_ref=src, dst_ref=dst, send_sem=send, recv_sem=recv, device_id=device_at(*peer), device_id_type=MESH
+    )
+
+
+def chunk_rows(rows, both, y, core):
+    if both:
+        return pl.ds(pl.multiple_of(core * (rows // 2), rows // 2), rows // 2)
+    return pl.ds(pl.multiple_of(core * (rows // 2) + y * (rows // 4), rows // 4), rows // 4)
+
+
+def core_rows(rows, core):
+    return pl.ds(pl.multiple_of(core * (rows // 2), rows // 2), rows // 2)
+
+
+class Gather:
+    AHEAD = 3
+
+    def __init__(self, shards, fulls, sems, depth):
+        self.shards, self.fulls, self.depth = shards, fulls, depth
+        (self.local_sem, self.z_send, self.z_recv, self.x_send, self.x_recv) = sems[:5]
+        (self.y_send, self.y_recv, self.c_send, self.c_recv) = sems[5:]
+        self.z, self.x, self.y, self.core = position()
+        self.count, self.now = len(GATHER_CHUNKS), 0
+
+    @staticmethod
+    def scratch(depth):
+        dma, count = pltpu.SemaphoreType.DMA, len(GATHER_CHUNKS)
+        return [dma((count,))] + [dma((count, depth - 1))] * 2 + [dma((count,))] * 6
+
+    def part(self, k):
+        tensor, lead, leads, both, column, columns = GATHER_CHUNKS[k]
+        rows = chunk_rows(self.shards[tensor].shape[1], both, self.y, self.core)
+        return self.fulls[tensor], pl.ds(lead, leads), rows, pl.ds(column, columns)
+
+    def place(self, k):
+        full, lead, rows, cols = self.part(k)
+        shard = self.shards[GATHER_CHUNKS[k][0]]
+        return pltpu.make_async_copy(
+            shard.at[lead, rows, cols], full.at[self.z, self.x, lead, rows, cols], self.local_sem.at[k]
+        )
+
+    def z_copies(self, k):
+        full, lead, rows, cols = self.part(k)
+        here = full.at[self.z, self.x, lead, rows, cols]
+        return [
+            remote(
+                here,
+                here,
+                self.z_send.at[k, step - 1],
+                self.z_recv.at[k, step - 1],
+                (lax.rem(self.z + step, self.depth), self.x, self.y, self.core),
+            )
+            for step in range(1, self.depth)
+        ]
+
+    def x_copy(self, k):
+        full, lead, rows, cols = self.part(k)
+        here = full.at[:, self.x, lead, rows, cols]
+        return remote(here, here, self.x_send.at[k], self.x_recv.at[k], (self.z, 1 - self.x, self.y, self.core))
+
+    def y_copy(self, k):
+        full, lead, rows, cols = self.part(k)
+        here = full.at[:, :, lead, rows, cols]
+        return remote(here, here, self.y_send.at[k], self.y_recv.at[k], (self.z, self.x, 1 - self.y, self.core))
+
+    def c_copy(self, k):
+        full, lead, _, cols = self.part(k)
+        here = full.at[:, :, lead, core_rows(full.shape[3], self.core), cols]
+        return remote(here, here, self.c_send.at[k], self.c_recv.at[k], (self.z, self.x, self.y, 1 - self.core))
+
+    def place_all(self):
+        for k in range(self.count):
+            self.place(k).start()
+
+    def launch(self, k):
+        if k < self.count:
+            self.place(k).wait()
+            for copy in self.z_copies(k):
+                copy.start()
+
+    def begin(self):
+        for k in range(self.AHEAD):
+            self.launch(k)
+
+    def tick(self):
+        now, count = self.now, self.count
+        self.now += 1
+        if now < count:
+            for copy in self.z_copies(now):
+                copy.wait_recv()
+            self.x_copy(now).start()
+            self.launch(now + self.AHEAD)
+        k = now - 1
+        if 0 <= k < count:
+            self.x_copy(k).wait_recv()
+            (self.c_copy if GATHER_CHUNKS[k][3] else self.y_copy)(k).start()
+        k = now - 2
+        if 0 <= k < count and not GATHER_CHUNKS[k][3]:
+            self.y_copy(k).wait_recv()
+            self.c_copy(k).start()
+        k = now - 3
+        if 0 <= k < count:
+            self.c_copy(k).wait_recv()
+
+    def pump(self, ticks=1):
+        for _ in range(ticks):
+            if self.now < self.count + 3:
+                self.tick()
+
+    def ready(self, tensor):
+        last = max(k for k, chunk in enumerate(GATHER_CHUNKS) if chunk[0] == tensor)
+        while self.now <= last + 3:
+            self.tick()
+
+    def close(self):
+        for k in range(self.count):
+            for copy in self.z_copies(k):
+                copy.wait_send()
+            self.x_copy(k).wait_send()
+            if not GATHER_CHUNKS[k][3]:
+                self.y_copy(k).wait_send()
+            self.c_copy(k).wait_send()
+
+
+def taps(tensor):
+    pieces = []
+    for lead in (0, 3, 6):
+        pieces += [(tensor, lead, 1, True, 0, 512), (tensor, lead + 1, 2, False, 0, 512)]
+    return pieces
+
+
+CHUNKS = (
+    [(0, 0, 1, False, column, 512) for column in (0, 512)],
+    taps(1),
+    [(2, lead, 1, False, 0, 256) for lead in (0, 1)],
+    [(3, lead, 1, lead == 0, 0, 256) for lead in range(4)],
+    [(4, 0, 1, column % 1024 == 0, column, 512) for column in (0, 512, 1024, 1536)],
+    taps(5),
+    [(6, lead, 1, False, 0, 256) for lead in (0, 1)],
+)
+GATHER_CHUNKS = [chunk for tensor in (0, 1, 3, 2, 4, 5, 6) for chunk in CHUNKS[tensor]]
+REDUCE_CHUNKS = [chunk for tensor in (6, 5, 4, 2, 3, 1, 0) for chunk in CHUNKS[tensor]]
+
+
+def add_blocks(extents, body):
+    total = 1
+    for extent in extents:
+        total *= extent
+
+    def step(flat, carry):
+        index = []
+        for extent in reversed(extents):
+            index.append(lax.rem(flat, extent))
+            flat = flat // extent
+        body(*reversed(index))
+        return carry
+
+    lax.fori_loop(0, total, step, 0)
+
+
+def add_to(target, source):
+    target[...] = (target[...].astype(jnp.float32) + source[...].astype(jnp.float32)).astype(jnp.bfloat16)
+
+
+class Reduce:
+    def __init__(self, held, outs, c_hbm, y_hbm, refs, depth):
+        self.held, self.outs, self.c_hbm, self.y_hbm, self.depth = held, outs, c_hbm, y_hbm, depth
+        self.count = len(REDUCE_CHUNKS)
+        refs = list(refs)
+
+        def take(count):
+            taken = refs[:count]
+            del refs[:count]
+            return taken
+
+        self.from_x, self.from_z, self.swap = take(self.count), take(self.count), take(self.count)
+        self.final = take(self.count)
+        self.c_tall, self.c_wide, self.y_tall, self.y_wide, self.squares = take(5)
+        self.c_sem, self.y_sem, self.x_sem, self.z_sem, self.s_sem, self.f_sem, self.q_sem, self.local_sem = take(8)
+        self.z, self.x, self.y, self.core = position()
+        self.now = self.enabled = 0
+
+    @staticmethod
+    def sizes(shapes):
+        for tensor, _, leads, both, _, columns in REDUCE_CHUNKS:
+            rows = shapes[tensor][3]
+            yield leads, rows, columns, rows // 2 if both else rows // 4, both
+
+    @staticmethod
+    def scratch(shapes, depth):
+        dma, count = pltpu.SemaphoreType.DMA, len(REDUCE_CHUNKS)
+        buffer = lambda *shape: pltpu.VMEM(shape, jnp.bfloat16)
+        sizes = list(Reduce.sizes(shapes))
+        return (
+            [buffer(depth, leads, part, columns) for leads, _, columns, part, _ in sizes]
+            + [buffer(depth - 1, leads, part, columns) for leads, _, columns, part, _ in sizes]
+            + [buffer(leads, part, columns) if both else buffer(16, 128) for leads, _, columns, part, both in sizes]
+            + [buffer(leads, rows, columns) for leads, rows, columns, _, _ in sizes]
+            + [buffer(2, depth, 2, 1, shapes[2][3] // 2, shapes[2][4]), buffer(2, depth, 2, 2, shapes[0][3] // 2, 512)]
+            + [buffer(2, depth, 2, 1, shapes[2][3] // 4, shapes[2][4]), buffer(2, depth, 2, 2, shapes[0][3] // 4, 512)]
+            + [pltpu.VMEM((2 * depth + 3, 8, 128), jnp.float32)]
+            + [dma((2, count))] * 3
+            + [dma((2, count, depth - 1)), dma((2, count)), dma((2, count, 3)), dma((2, depth)), dma((3, count))]
+        )
+
+    def piece(self, k):
+        tensor, lead, leads, both, column, columns = REDUCE_CHUNKS[k]
+        held = self.held[tensor]
+        rows = held.shape[3]
+        return held, rows, pl.ds(lead, leads), pl.ds(column, columns), chunk_rows(rows, both, self.y, self.core)
+
+    def extents(self, k):
+        return REDUCE_CHUNKS[k][2], REDUCE_CHUNKS[k][1]
+
+    def slot(self, k, tall, wide):
+        tensor, _, leads = REDUCE_CHUNKS[k][:3]
+        buffer = tall if tensor in (2, 3, 6) else wide
+        return buffer.at[k % 2, :, :, pl.ds(0, leads)]
+
+    def c_copy(self, k):
+        held, rows, lead, cols, _ = self.piece(k)
+        return remote(
+            held.at[:, :, lead, core_rows(rows, 1 - self.core), cols],
+            self.c_hbm[REDUCE_CHUNKS[k][0]].at[:, :, lead, :, cols],
+            self.c_sem.at[0, k],
+            self.c_sem.at[1, k],
+            (self.z, self.x, self.y, 1 - self.core),
+        )
+
+    def c_load(self, k):
+        _, _, lead, cols, _ = self.piece(k)
+        return pltpu.make_async_copy(
+            self.c_hbm[REDUCE_CHUNKS[k][0]].at[:, :, lead, :, cols],
+            self.slot(k, self.c_tall, self.c_wide),
+            self.local_sem.at[0, k],
+        )
+
+    def y_copy(self, k):
+        held, rows, lead, cols, _ = self.piece(k)
+        return remote(
+            held.at[:, :, lead, chunk_rows(rows, False, 1 - self.y, self.core), cols],
+            self.y_hbm[REDUCE_CHUNKS[k][0]].at[:, :, lead, :, cols],
+            self.y_sem.at[0, k],
+            self.y_sem.at[1, k],
+            (self.z, self.x, 1 - self.y, self.core),
+        )
+
+    def y_load(self, k):
+        _, _, lead, cols, _ = self.piece(k)
+        return pltpu.make_async_copy(
+            self.y_hbm[REDUCE_CHUNKS[k][0]].at[:, :, lead, :, cols],
+            self.slot(k, self.y_tall, self.y_wide),
+            self.local_sem.at[1, k],
+        )
+
+    def x_copy(self, k):
+        held, _, lead, cols, rows = self.piece(k)
+        return remote(
+            held.at[:, 1 - self.x, lead, rows, cols],
+            self.from_x[k],
+            self.x_sem.at[0, k],
+            self.x_sem.at[1, k],
+            (self.z, 1 - self.x, self.y, self.core),
+        )
+
+    def z_copies(self, k):
+        held, _, lead, cols, rows = self.piece(k)
+        copies = []
+        for step in range(1, self.depth):
+            there = lax.rem(self.z + step, self.depth)
+            copies.append(
+                remote(
+                    held.at[there, self.x, lead, rows, cols],
+                    self.from_z[k].at[step - 1],
+                    self.z_sem.at[0, k, step - 1],
+                    self.z_sem.at[1, k, step - 1],
+                    (there, self.x, self.y, self.core),
+                )
+            )
+        return copies
+
+    def s_copy(self, k):
+        rows = self.piece(k)[4]
+        return remote(
+            self.final[k].at[:, rows],
+            self.swap[k],
+            self.s_sem.at[0, k],
+            self.s_sem.at[1, k],
+            (self.z, self.x, 1 - self.y, self.core),
+        )
+
+    def f_copies(self, k):
+        here = self.final[k].at[:, self.piece(k)[4]]
+        peers = [(self.z, self.x, self.y, 1 - self.core)]
+        if not REDUCE_CHUNKS[k][3]:
+            peers += [(self.z, self.x, 1 - self.y, self.core), (self.z, self.x, 1 - self.y, 1 - self.core)]
+        return [
+            remote(here, here, self.f_sem.at[0, k, i], self.f_sem.at[1, k, i], peer) for i, peer in enumerate(peers)
+        ]
+
+    def store(self, k):
+        tensor = REDUCE_CHUNKS[k][0]
+        _, _, lead, cols, _ = self.piece(k)
+        return pltpu.make_async_copy(self.final[k], self.outs[tensor].at[lead, :, cols], self.local_sem.at[2, k])
+
+    def add_c(self, k):
+        held, rows, _, cols, _ = self.piece(k)
+        leads, lead = self.extents(k)
+        half, slot = core_rows(rows, self.core), self.slot(k, self.c_tall, self.c_wide)
+        add_blocks(
+            (self.depth, 2, leads), lambda z, x, i: add_to(held.at[z, x, lead + i, half, cols], slot.at[z, x, i])
+        )
+
+    def add_y(self, k):
+        held, _, _, cols, rows = self.piece(k)
+        leads, lead = self.extents(k)
+        slot = self.slot(k, self.y_tall, self.y_wide)
+        add_blocks(
+            (self.depth, 2, leads), lambda z, x, i: add_to(held.at[z, x, lead + i, rows, cols], slot.at[z, x, i])
+        )
+
+    def add_x(self, k):
+        held, _, _, cols, rows = self.piece(k)
+        leads, lead = self.extents(k)
+        add_blocks(
+            (self.depth, leads), lambda z, i: add_to(held.at[z, self.x, lead + i, rows, cols], self.from_x[k].at[z, i])
+        )
+
+    def add_z(self, k):
+        held, _, _, cols, rows = self.piece(k)
+        leads, lead = self.extents(k)
+
+        def body(i):
+            total = held[self.z, self.x, lead + i, rows, cols].astype(jnp.float32)
+            for step in range(1, self.depth):
+                total = total + self.from_z[k][step - 1, i].astype(jnp.float32)
+            self.final[k][i, rows] = total.astype(jnp.bfloat16)
+
+        add_blocks((leads,), body)
+
+    def add_s(self, k):
+        rows = self.piece(k)[4]
+        add_blocks((self.extents(k)[0],), lambda i: add_to(self.final[k].at[i, rows], self.swap[k].at[i]))
+
+    def add_squares(self, k):
+        leads = self.extents(k)[0]
+        lanes = lax.broadcasted_iota(jnp.int32, (8, 128), 1)
+        subs = lax.broadcasted_iota(jnp.int32, (8, 128), 0)
+        where = (subs == 1) & (lanes == REDUCE_CHUNKS[k][0])
+
+        def body(i):
+            block = self.final[k][i].astype(jnp.float32)
+            total = jnp.sum(jnp.sum(block * block, axis=0, keepdims=True), axis=1, keepdims=True)
+            self.squares[2 * self.depth + 2] += jnp.where(where, total, 0.0)
+
+        add_blocks((leads,), body)
+
+    STAGES = 9
+
+    def stage(self, k, number):
+        both = REDUCE_CHUNKS[k][3]
+        if number == 0:
+            self.c_copy(k).start()
+        elif number == 1:
+            self.c_copy(k).wait_recv()
+            self.c_load(k).start()
+        elif number == 2:
+            self.c_load(k).wait()
+            self.add_c(k)
+            (self.x_copy if both else self.y_copy)(k).start()
+        elif number == 3 and not both:
+            self.y_copy(k).wait_recv()
+            self.y_load(k).start()
+        elif number == 4 and not both:
+            self.y_load(k).wait()
+            self.add_y(k)
+            self.x_copy(k).start()
+        elif number == 5:
+            self.x_copy(k).wait_recv()
+            self.add_x(k)
+            for copy in self.z_copies(k):
+                copy.start()
+        elif number == 6:
+            for copy in self.z_copies(k):
+                copy.wait_recv()
+            self.add_z(k)
+            for copy in [self.s_copy(k)] if both else self.f_copies(k):
+                copy.start()
+        elif number == 7 and both:
+            self.s_copy(k).wait_recv()
+            self.s_copy(k).wait_send()
+            self.add_s(k)
+            for copy in self.f_copies(k):
+                copy.start()
+        elif number == 8:
+            for copy in self.f_copies(k):
+                copy.wait_recv()
+            self.store(k).start()
+            self.add_squares(k)
+
+    def enable(self, tensor, leads_done=None):
+        while self.enabled < self.count:
+            chunk = REDUCE_CHUNKS[self.enabled]
+            if chunk[0] != tensor or (leads_done is not None and chunk[1] + chunk[2] > leads_done):
+                break
+            self.enabled += 1
+
+    def pump(self, ticks=1):
+        for _ in range(ticks):
+            if self.now < self.enabled or (self.enabled == self.count and self.now < self.count + self.STAGES):
+                for number in reversed(range(self.STAGES)):
+                    k = self.now - number
+                    if 0 <= k < self.count:
+                        self.stage(k, number)
+                self.now += 1
+
+    def finish(self, weight_squares, sums_out):
+        while self.now < self.count + self.STAGES:
+            self.pump()
+        squares, depth = self.squares, self.depth
+        subs = lax.broadcasted_iota(jnp.int32, (8, 128), 0)
+        mine = squares.at[self.z * 2 + self.x]
+        mine[...] = squares[2 * depth + 2] + jnp.where(subs == 0, weight_squares[...], 0.0)
+        copies = [
+            remote(
+                mine,
+                mine,
+                self.q_sem.at[0, step],
+                self.q_sem.at[1, step],
+                (lax.rem(self.z + step, depth), self.x, self.y, self.core),
+            )
+            for step in range(1, depth)
+        ]
+        for copy in copies:
+            copy.start()
+        for copy in copies:
+            copy.wait_recv()
+        own = squares[self.x]
+        for deep in range(1, depth):
+            own = own + squares[deep * 2 + self.x]
+        column = squares.at[2 * depth + self.x]
+        column[...] = own
+        across = remote(
+            column, column, self.q_sem.at[0, 0], self.q_sem.at[1, 0], (self.z, 1 - self.x, self.y, self.core)
+        )
+        across.start()
+        across.wait_recv()
+        sums_out[...] = squares[2 * depth] + squares[2 * depth + 1]
+        across.wait_send()
+        for copy in copies:
+            copy.wait_send()
+        for k in range(self.count):
+            self.c_copy(k).wait_send()
+            if not REDUCE_CHUNKS[k][3]:
+                self.y_copy(k).wait_send()
+            self.x_copy(k).wait_send()
+            for copy in self.z_copies(k) + self.f_copies(k):
+                copy.wait_send()
+            self.store(k).wait()
+
+
+class NearFar:
+    def __init__(self, refs, depth):
+        self.near, self.far, self.total, self.near_send, self.near_recv, self.far_send, self.far_recv = refs
+        self.depth = depth
+        self.z, self.x, self.y, self.core = position()
+        self.mine = self.x * 4 + self.y * 2 + self.core
+        self.pay = self.near.at[self.mine]
+        self.sent = []
+
+    @staticmethod
+    def scratch(width, depth):
+        dma = pltpu.SemaphoreType.DMA
+        return [
+            pltpu.VMEM((8, 8, width), jnp.float32),
+            pltpu.VMEM((depth, 8, width), jnp.float32),
+            pltpu.VMEM((8, width), jnp.float32),
+            dma((7,)),
+            dma((7,)),
+            dma((depth - 1,)),
+            dma((depth - 1,)),
+        ]
+
+    def near_copies(self):
+        copies = []
+        for offset in range(1, 8):
+            x = 1 - self.x if offset & 4 else self.x
+            y = 1 - self.y if offset & 2 else self.y
+            core = 1 - self.core if offset & 1 else self.core
+            here = self.near.at[self.mine]
+            copies.append(
+                remote(here, here, self.near_send.at[offset - 1], self.near_recv.at[offset - 1], (self.z, x, y, core))
+            )
+        return copies
+
+    def far_copies(self):
+        here = self.far.at[self.z]
+        return [
+            remote(
+                here,
+                here,
+                self.far_send.at[step - 1],
+                self.far_recv.at[step - 1],
+                (lax.rem(self.z + step, self.depth), self.x, self.y, self.core),
+            )
+            for step in range(1, self.depth)
+        ]
+
+    def begin(self):
+        for copy in self.near_copies():
+            copy.start()
+
+    def stages(self):
+        def middle():
+            for copy in self.near_copies():
+                copy.wait_recv()
+            total = self.near[0]
+            for slot in range(1, 8):
+                total = total + self.near[slot]
+            self.far[self.z] = total
+            for copy in self.far_copies():
+                copy.start()
+
+        def last():
+            for copy in self.far_copies():
+                copy.wait_recv()
+            total = self.far[0]
+            for slot in range(1, self.depth):
+                total = total + self.far[slot]
+            self.total[...] = total
+
+        return [middle, last]
+
+    def close(self):
+        for copy in self.near_copies() + self.far_copies():
+            copy.wait_send()
+
+
+class Split:
+    def __init__(self, refs, depth):
+        (self.pay, self.half, self.quad, self.deep, self.total, self.c_send, self.c_recv) = refs[:7]
+        (self.q_send, self.q_recv, self.z_send, self.z_recv, self.g_send, self.g_recv) = refs[7:]
+        self.depth = depth
+        self.z, self.x, self.y, self.core = position()
+        self.width = self.pay.shape[1]
+        self.mine = self.x * 2 + self.y
+
+    @staticmethod
+    def scratch(width, depth):
+        dma = pltpu.SemaphoreType.DMA
+        return [
+            pltpu.VMEM((8, width), jnp.float32),
+            pltpu.VMEM((8, width // 2), jnp.float32),
+            pltpu.VMEM((4, 8, width // 8), jnp.float32),
+            pltpu.VMEM((depth, 8, width // 8), jnp.float32),
+            pltpu.VMEM((8, width), jnp.float32),
+            dma((2,)),
+            dma((2,)),
+            dma((3,)),
+            dma((3,)),
+            dma((depth - 1,)),
+            dma((depth - 1,)),
+            dma((3,)),
+            dma((3,)),
+        ]
+
+    def half_of(self, core):
+        return pl.ds(pl.multiple_of(core * (self.width // 2), 128), self.width // 2)
+
+    def eighth_of(self, slot):
+        start = self.core * (self.width // 2) + slot * (self.width // 8)
+        return pl.ds(pl.multiple_of(start, 128), self.width // 8)
+
+    def core_copy(self):
+        return remote(
+            self.pay.at[:, self.half_of(1 - self.core)],
+            self.half,
+            self.c_send.at[0],
+            self.c_recv.at[0],
+            (self.z, self.x, self.y, 1 - self.core),
+        )
+
+    def around(self):
+        for offset in range(1, 4):
+            x = 1 - self.x if offset & 2 else self.x
+            y = 1 - self.y if offset & 1 else self.y
+            yield offset - 1, x, y
+
+    def quad_copies(self):
+        return [
+            remote(
+                self.pay.at[:, self.eighth_of(x * 2 + y)],
+                self.quad.at[self.mine],
+                self.q_send.at[i],
+                self.q_recv.at[i],
+                (self.z, x, y, self.core),
+            )
+            for i, x, y in self.around()
+        ]
+
+    def deep_copies(self):
+        here = self.deep.at[self.z]
+        return [
+            remote(
+                here,
+                here,
+                self.z_send.at[step - 1],
+                self.z_recv.at[step - 1],
+                (lax.rem(self.z + step, self.depth), self.x, self.y, self.core),
+            )
+            for step in range(1, self.depth)
+        ]
+
+    def gather_copies(self):
+        here = self.total.at[:, self.eighth_of(self.mine)]
+        return [
+            remote(here, here, self.g_send.at[i], self.g_recv.at[i], (self.z, x, y, self.core))
+            for i, x, y in self.around()
+        ]
+
+    def last_copy(self):
+        here = self.total.at[:, self.half_of(self.core)]
+        return remote(here, here, self.c_send.at[1], self.c_recv.at[1], (self.z, self.x, self.y, 1 - self.core))
+
+    def begin(self):
+        self.core_copy().start()
+
+    def stages(self):
+        def first():
+            self.core_copy().wait_recv()
+            half = self.half_of(self.core)
+            self.pay[:, half] = self.pay[:, half] + self.half[...]
+            for copy in self.quad_copies():
+                copy.start()
+            self.quad[self.mine] = self.pay[:, self.eighth_of(self.mine)]
+
+        def second():
+            for copy in self.quad_copies():
+                copy.wait_recv()
+            self.deep[self.z] = (self.quad[0] + self.quad[1]) + (self.quad[2] + self.quad[3])
+            for copy in self.deep_copies():
+                copy.start()
+
+        def third():
+            for copy in self.deep_copies():
+                copy.wait_recv()
+            total = self.deep[0]
+            for slot in range(1, self.depth):
+                total = total + self.deep[slot]
+            self.total[:, self.eighth_of(self.mine)] = total
+            for copy in self.gather_copies():
+                copy.start()
+
+        def fourth():
+            for copy in self.gather_copies():
+                copy.wait_recv()
+            self.last_copy().start()
+
+        def fifth():
+            self.last_copy().wait_recv()
+            for copy in self.gather_copies() + [self.last_copy()]:
+                copy.wait_send()
+
+        return [first, second, third, fourth, fifth]
+
+    def close(self):
+        self.core_copy().wait_send()
+        for copy in self.quad_copies() + self.deep_copies():
+            copy.wait_send()
+
+
+def interleave(stages, works):
+    done = 0
+    for i, stage in enumerate(stages):
+        upto = (len(works) * (i + 1)) // len(stages)
+        for work in works[done:upto]:
+            work()
+        done = upto
+        stage()
+
+
+HAT_A1, HAT_A2, HAT_A3, HAT_AS, HAT_B1, HAT_B2, HAT_B3, PATCH_A, PATCH_B, ACT_A2, ACT_B2, OUT_A = SAVED = range(12)
+NORMS_MID, NORMS_OUT, SUM_A1, SUM_A2, SUM_A3, SUM_AS, SUM_B1, SUM_B2, SUM_B3, SUM_J = range(10)
+
+
+def columns(j):
+    return pl.ds(pl.multiple_of(j * 128, 128), 128)
+
+
+def dot(a, b):
+    return lax.dot_general(a, b, (((1,), (0,)), ((), ())), preferred_element_type=jnp.float32)
+
+
+def dot_nt(a, b):
+    return lax.dot_general(a, b, (((1,), (1,)), ((), ())), preferred_element_type=jnp.float32)
+
+
+def sigmoid(v):
+    return 0.5 * jnp.tanh(0.5 * v) + 0.5
+
+
+def slope(v):
+    s = sigmoid(v)
+    return s * (1.0 + v * (1.0 - s))
+
+
+class Plan:
+    def __init__(self, shapes):
+        self.sides = [shape[1] // 2 for shape in shapes]
+        self.slots = [shape[0] for shape in shapes]
+        self.valid = [side * side * slots for side, slots in zip(self.sides, self.slots)]
+        sizes = [-(-valid // 8) * 8 for valid in self.valid]
+        sizes[2] += -sum(sizes) % 128
+        self.starts = [0, sizes[0], sizes[0] + sizes[1]]
+        self.sizes = sizes
+        self.rows = sum(sizes)
+
+    def spans(self):
+        return [slice(start, start + size) for start, size in zip(self.starts, self.sizes)]
+
+    def shifts(self):
+        out = np.zeros((9, self.rows, self.rows), np.float32)
+        for side, slots, start in zip(self.sides, self.slots, self.starts):
+            at = lambda i, j, n: start + (i * side + j) * slots + n
+            for di in (-1, 0, 1):
+                for dj in (-1, 0, 1):
+                    for i in range(max(0, -di), min(side, side - di)):
+                        for j in range(max(0, -dj), min(side, side - dj)):
+                            for n in range(slots):
+                                out[(di + 1) * 3 + dj + 1, at(i, j, n), at(i + di, j + dj, n)] = 1.0
+        return out.astype(jnp.bfloat16)
+
+
+def put_sums(plan, pairs, mask, pay, base, width):
+    def body(j, carry):
+        firsts, seconds = [0.0] * 3, [0.0] * 3
+        for first, second in pairs(j):
+            for g, span in enumerate(plan.spans()):
+                live = first[span] * mask[span, :]
+                firsts[g] = firsts[g] + jnp.sum(live, axis=0, keepdims=True)
+                seconds[g] = seconds[g] + jnp.sum(live * second[span], axis=0, keepdims=True)
+        zero = jnp.zeros((1, 128), jnp.float32)
+        pay[:, columns(base + j)] = jnp.concatenate(firsts + seconds + [zero, zero], axis=0)
+        return carry
+
+    lax.fori_loop(0, width // 128, body, 0)
+
+
+def put_scales(total, inverse, over, width, factor=1.0):
+    def body(j, carry):
+        at = columns(j)
+        per = over[0:3, :] * factor
+        means = total[0:3, at] * per
+        variance = total[3:6, at] * per - means * means
+        scales = lax.rsqrt(variance + EPSILON)
+        zero = jnp.zeros((5, 128), jnp.float32)
+        total[:, at] = jnp.concatenate([means, zero], axis=0)
+        inverse[:, at] = jnp.concatenate([scales, zero], axis=0)
+        return carry
+
+    lax.fori_loop(0, width // 128, body, 0)
+
+
+def by_group(plan, of):
+    return jnp.concatenate([of(g, span) for g, span in enumerate(plan.spans())], axis=0)
+
+
+def forward_names(depth):
+    return (
+        (NORMS_MID, NearFar.scratch(512, depth)),
+        (NORMS_OUT, Split.scratch(2048, depth)),
+        (SUM_A1, NearFar.scratch(512, depth)),
+        (SUM_A2, NearFar.scratch(512, depth)),
+        (SUM_AS, Split.scratch(2048, depth)),
+        (SUM_A3, Split.scratch(2048, depth)),
+        (SUM_B1, NearFar.scratch(512, depth)),
+        (SUM_B2, NearFar.scratch(512, depth)),
+        (SUM_B3, Split.scratch(2048, depth)),
+    )
+
+
+def forward_kernel(plan, depth, *refs):
+    refs = list(refs)
+
+    def take(count):
+        taken = refs[:count]
+        del refs[:count]
+        return taken
+
+    x_hbm, shift_hbm, mask, counts, norm_mid, norm_out = take(6)
+    shards = take(7)
+    out, inv_mid, inv_out, par_mid, par_out, over = take(6)
+    weights_hbm = take(7)
+    saved_hbm = dict(zip(SAVED, take(len(SAVED))))
+    sums = {}
+    for name, scratch in forward_names(depth):
+        sums[name] = (NearFar if len(scratch) == 7 else Split)(take(len(scratch)), depth)
+    x, shift = take(2)
+    w_a1, w_a2, w_a3, w_as, w_b1, w_b2, w_b3 = weights = take(7)
+    saved = dict(zip(SAVED, take(len(SAVED))))
+    hid_a1, hid_mid, hid_out, hid_as, act = take(5)
+    load_sem, save_sem, full_sem = take(3)
+    gather = Gather(shards, weights, take(9), depth)
+
+    loads = [
+        pltpu.make_async_copy(src, dst, load_sem.at[i])
+        for i, (src, dst) in enumerate(zip([x_hbm, shift_hbm], [x, shift]))
+    ]
+    gather.place_all()
+    for copy in loads:
+        copy.start()
+
+    def keep(i):
+        return pltpu.make_async_copy(weights[i], weights_hbm[i], full_sem.at[i])
+
+    def ready(i):
+        gather.ready(i)
+        keep(i).start()
+
+    def pump():
+        gather.pump()
+
+    def save(name):
+        pltpu.make_async_copy(saved[name], saved_hbm[name], save_sem.at[SAVED.index(name)]).start()
+
+    greet(depth)
+    gather.begin()
+    sums[NORMS_MID].pay[...] = norm_mid[...]
+    sums[NORMS_MID].begin()
+    sums[NORMS_OUT].pay[...] = norm_out[...]
+    sums[NORMS_OUT].begin()
+    norms_mid_stages = sums[NORMS_MID].stages()
+    norms_out_stages = sums[NORMS_OUT].stages()
+    rows = plan.rows
+
+    loads[0].wait()
+    norms_mid_stages[0]()
+    norms_out_stages[0]()
+    ready(0)
+
+    def conv_a1(p, carry):
+        hid_a1[p] = dot_nt(x[p], w_a1[...].reshape(512, -1))
+        return carry
+
+    lax.fori_loop(0, 2, conv_a1, 0)
+    norms_mid_stages[1]()
+    norms_out_stages[1]()
+    pump()
+    lax.fori_loop(2, 4, conv_a1, 0)
+    par_mid[...] = sums[NORMS_MID].total[...]
+    norms_out_stages[2]()
+
+    total = sums[SUM_A1]
+    put_sums(
+        plan, lambda j: [(hid_a1[p, :, columns(j)],) * 2 for p in range(4)], mask, total.pay, 0, 512
+    )
+    total.pay[6:7, 0:128] = counts[...]
+    total.begin()
+    pump()
+    total.stages()[0]()
+    norms_out_stages[3]()
+    pump()
+    total.stages()[1]()
+    norms_out_stages[4]()
+    par_out[...] = sums[NORMS_OUT].total[...]
+
+    pixels = total.total[6:7, 0:128]
+    lanes = lax.broadcasted_iota(jnp.int32, (1, 128), 1)
+    inverse_counts = [
+        jnp.broadcast_to(1.0 / jnp.sum(jnp.where(lanes == g, pixels, 0.0), axis=1, keepdims=True), (1, 128))
+        for g in range(3)
+    ]
+    over[...] = jnp.concatenate(inverse_counts + [jnp.zeros((5, 128), jnp.float32)], axis=0)
+    put_scales(total.total, inv_mid.at[0], over, 512, 0.25)
+
+    def normalized(hidden, total, inverse, hat, params, row, j):
+        at = columns(j)
+        xhat = by_group(plan, lambda g, span: (hidden[span] - total[g : g + 1, at]) * inverse[g : g + 1, at])
+        hat[:, at] = xhat.astype(jnp.bfloat16)
+        return xhat * params[row : row + 1, at] + params[row + 1 : row + 2, at]
+
+    def activate(hidden_of, total, inverse, hat, params, row, target):
+        def body(j, carry):
+            v = normalized(hidden_of(j), total, inverse, hat, params, row, j)
+            target[:, columns(j)] = (v * sigmoid(v)).astype(jnp.bfloat16)
+            return carry
+
+        lax.fori_loop(0, 4, body, 0)
+
+    def activate_a1(p, carry):
+        activate(
+            lambda j: hid_a1[p, :, columns(j)],
+            total.total,
+            inv_mid.at[0],
+            saved[HAT_A1].at[p],
+            par_mid,
+            0,
+            act.at[p],
+        )
+        return carry
+
+    lax.fori_loop(0, 2, activate_a1, 0)
+    pump()
+    lax.fori_loop(2, 4, activate_a1, 0)
+    save(HAT_A1)
+
+    loads[1].wait()
+    patch = saved[PATCH_A]
+    for tap in range(9):
+        a, b = tap // 3, tap % 3
+        plane = (0 if a == 1 else 2) + (0 if b == 1 else 1)
+        matrix = (0 if a == 0 else 1) * 3 + (0 if b == 0 else 1)
+        if matrix == 4:
+            patch[tap] = act[plane]
+        else:
+            patch[tap] = dot(shift[matrix], act[plane]).astype(jnp.bfloat16)
+        if tap == 4:
+            pump()
+    save(PATCH_A)
+    ready(1)
+
+    def spatial(patch, weight):
+        hid_mid[...] = dot_nt(patch[0], weight[:, :, 0].reshape(512, 512))
+
+        def body(tap, carry):
+            hid_mid[...] += dot_nt(patch[tap], weight[:, :, tap].reshape(512, 512))
+            return carry
+
+        lax.fori_loop(1, 9, body, 0)
+
+    spatial(patch, w_a2)
+
+    def conv_as(d, carry):
+        at = pl.ds(pl.multiple_of(d * 256, 256), 256)
+        hid_as[:, at] = dot(x[0], w_as[d // 2, lax.rem(d, 2)].reshape(1024, 256))
+        return carry
+
+    def shortcut():
+        ready(3)
+        lax.fori_loop(0, 8, conv_as, 0)
+        put_sums(plan, lambda j: [(hid_as[:, columns(j)],) * 2], mask, sums[SUM_AS].pay, 0, 2048)
+        sums[SUM_AS].begin()
+
+    as_stages = sums[SUM_AS].stages()
+
+    def mid_sums(total, name_index, works):
+        put_sums(plan, lambda j: [(hid_mid[:, columns(j)],) * 2], mask, total.pay, 0, 512)
+        total.begin()
+        interleave(total.stages(), works)
+        put_scales(total.total, inv_mid.at[name_index], over, 512)
+
+    mid_sums(sums[SUM_A2], 1, [pump, pump])
+    activate(
+        lambda j: hid_mid[:, columns(j)], sums[SUM_A2].total, inv_mid.at[1], saved[HAT_A2], par_mid, 2, saved[ACT_A2]
+    )
+    save(HAT_A2)
+    save(ACT_A2)
+
+    def expand(act_ref, weight):
+        def body(d, carry):
+            at = pl.ds(pl.multiple_of(d * 256, 256), 256)
+            hid_out[:, at] = dot(act_ref[...], weight[d // 2, lax.rem(d, 2)].reshape(512, 256))
+            return carry
+
+        lax.fori_loop(0, 8, body, 0)
+
+    def out_sums(total, name_index, works):
+        put_sums(plan, lambda j: [(hid_out[:, columns(j)],) * 2], mask, total.pay, 0, 2048)
+        total.begin()
+        interleave(total.stages(), works)
+        put_scales(total.total, inv_out.at[name_index], over, 2048)
+
+    shortcut()
+    as_stages[0]()
+    ready(2)
+    as_stages[1]()
+    expand(saved[ACT_A2], w_a3)
+    as_stages[2]()
+    out_sums(sums[SUM_A3], 0, [as_stages[3], pump, as_stages[4], pump, pump])
+    put_scales(sums[SUM_AS].total, inv_out.at[1], over, 2048)
+
+    def join(j, carry):
+        at = columns(j)
+        v = normalized(hid_out[:, at], sums[SUM_A3].total, inv_out.at[0], saved[HAT_A3], par_out, 0, j)
+        v = v + normalized(hid_as[:, at], sums[SUM_AS].total, inv_out.at[1], saved[HAT_AS], par_out, 2, j)
+        saved[OUT_A][:, at] = (v * sigmoid(v) * mask[...]).astype(jnp.bfloat16)
+        return carry
+
+    lax.fori_loop(0, 16, join, 0)
+    for name in (HAT_A3, HAT_AS, OUT_A):
+        save(name)
+
+    ready(4)
+    hid_mid[...] = dot_nt(saved[OUT_A][...], w_b1[...].reshape(512, -1))
+    mid_sums(sums[SUM_B1], 2, [pump, pump])
+    activate(
+        lambda j: hid_mid[:, columns(j)], sums[SUM_B1].total, inv_mid.at[2], saved[HAT_B1], par_mid, 4, act.at[0]
+    )
+    save(HAT_B1)
+
+    def patches(tap, carry):
+        saved[PATCH_B][tap] = dot(shift[tap], act[0]).astype(jnp.bfloat16)
+        return carry
+
+    lax.fori_loop(0, 9, patches, 0)
+    save(PATCH_B)
+    ready(5)
+    spatial(saved[PATCH_B], w_b2)
+    mid_sums(sums[SUM_B2], 3, [pump, pump])
+    activate(
+        lambda j: hid_mid[:, columns(j)], sums[SUM_B2].total, inv_mid.at[3], saved[HAT_B2], par_mid, 6, saved[ACT_B2]
+    )
+    save(HAT_B2)
+    save(ACT_B2)
+    ready(6)
+    expand(saved[ACT_B2], w_b3)
+    out_sums(sums[SUM_B3], 2, [])
+
+    def finish(j, carry):
+        at = columns(j)
+        v = normalized(hid_out[:, at], sums[SUM_B3].total, inv_out.at[2], saved[HAT_B3], par_out, 4, j)
+        v = v + saved[OUT_A][:, at].astype(jnp.float32)
+        out[:, at] = (v * sigmoid(v) * mask[...]).astype(jnp.bfloat16)
+        return carry
+
+    lax.fori_loop(0, 16, finish, 0)
+    save(HAT_B3)
+    for total in sums.values():
+        total.close()
+    for i, name in enumerate(SAVED):
+        pltpu.make_async_copy(saved[name], saved_hbm[name], save_sem.at[i]).wait()
+    gather.close()
+    for i in range(7):
+        keep(i).wait()
+
+
+def saved_shapes(rows):
+    bf16 = jnp.bfloat16
+    return (
+        ((4, rows, 512), bf16),
+        ((rows, 512), bf16),
+        ((rows, 2048), bf16),
+        ((rows, 2048), bf16),
+        ((rows, 512), bf16),
+        ((rows, 512), bf16),
+        ((rows, 2048), bf16),
+        ((9, rows, 512), bf16),
+        ((9, rows, 512), bf16),
+        ((rows, 512), bf16),
+        ((rows, 512), bf16),
+        ((rows, 2048), bf16),
+    )
+
+
+WHOLE = pl.BlockSpec(memory_space=pltpu.VMEM)
+VMEM_LIMIT = 62 * 1024 * 1024
+
+
+def run_forward(plan, depth, x, shifts, mask, counts, norm_mid, norm_out, shards):
+    rows, f32, bf16 = plan.rows, jnp.float32, jnp.bfloat16
+    dma = pltpu.SemaphoreType.DMA
+    scratch = []
+    for _, pieces in forward_names(depth):
+        scratch += pieces
+    scratch += [pltpu.VMEM(x.shape, bf16), pltpu.VMEM(shifts.shape, bf16)]
+    fulls = [jax.ShapeDtypeStruct((depth, 2, *shard.shape), bf16) for shard in shards]
+    scratch += [pltpu.VMEM(full.shape, bf16) for full in fulls]
+    scratch += [pltpu.VMEM(shape, kind) for shape, kind in saved_shapes(rows)]
+    scratch += [
+        pltpu.VMEM((4, rows, 512), f32),
+        pltpu.VMEM((rows, 512), f32),
+        pltpu.VMEM((rows, 2048), f32),
+        pltpu.VMEM((rows, 2048), f32),
+        pltpu.VMEM((4, rows, 512), bf16),
+        dma((2,)),
+        dma((len(SAVED),)),
+        dma((7,)),
+    ]
+    scratch += Gather.scratch(depth)
+    small = [
+        jax.ShapeDtypeStruct((rows, 2048), bf16),
+        jax.ShapeDtypeStruct((4, 8, 512), f32),
+        jax.ShapeDtypeStruct((3, 8, 2048), f32),
+        jax.ShapeDtypeStruct((8, 512), f32),
+        jax.ShapeDtypeStruct((8, 2048), f32),
+        jax.ShapeDtypeStruct((8, 128), f32),
+    ]
+    return pl.pallas_call(
+        functools.partial(forward_kernel, plan, depth),
+        out_shape=small + fulls + [jax.ShapeDtypeStruct(shape, kind) for shape, kind in saved_shapes(rows)],
+        in_specs=[ANY, ANY] + [WHOLE] * 4 + [ANY] * 7,
+        out_specs=[WHOLE] * 6 + [ANY] * 7 + [ANY] * len(SAVED),
+        scratch_shapes=scratch,
+        compiler_params=pltpu.CompilerParams(collective_id=0, has_side_effects=True, vmem_limit_bytes=VMEM_LIMIT),
+    )(x, shifts, mask, counts, norm_mid, norm_out, *shards)
+
+
+def backward_names(depth):
+    return (
+        (SUM_B3, Split.scratch(2048, depth)),
+        (SUM_B2, NearFar.scratch(512, depth)),
+        (SUM_B1, NearFar.scratch(512, depth)),
+        (SUM_J, Split.scratch(4096, depth)),
+        (SUM_A2, NearFar.scratch(512, depth)),
+        (SUM_A1, NearFar.scratch(512, depth)),
+    )
+
+
+def backward_kernel(plan, depth, *refs):
+    refs = list(refs)
+
+    def take(count):
+        taken = refs[:count]
+        del refs[:count]
+        return taken
+
+    x_hbm, shift_hbm, cot_hbm, mask, weight_squares, inv_mid, inv_out, par_mid, par_out, over = take(10)
+    saved_hbm = dict(zip(SAVED, take(len(SAVED))))
+    weights_hbm = take(7)
+    dx_hbm, pgrad_mid, pgrad_b3, pgrad_j, squares_out = take(5)
+    gradients_hbm, c_hbm, y_hbm = take(7), take(7), take(7)
+    sums = {}
+    for name, scratch in backward_names(depth):
+        sums[name] = (NearFar if len(scratch) == 7 else Split)(take(len(scratch)), depth)
+    x, shift, cot = take(3)
+    w_a1, w_a2, w_a3, w_as, w_b1, w_b2, w_b3 = weights = take(7)
+    kept = [name for name in SAVED if name != PATCH_B]
+    saved = dict(zip(kept, take(len(kept))))
+    saved[PATCH_B] = saved[PATCH_A]
+    dz, dact, dh_mid, flip = take(4)
+    load_sem, saved_sem, dx_sem = take(3)
+    dh_a, dh_b = cot, saved[HAT_B3]
+    planes = [saved[HAT_AS].at[:, pl.ds(plane * 512, 512)] for plane in range(4)]
+    reduce = Reduce(weights, gradients_hbm, c_hbm, y_hbm, refs, depth)
+    reduce.squares[2 * depth + 2] = jnp.zeros((8, 128), jnp.float32)
+
+    def pump():
+        reduce.pump()
+
+    def loading(name):
+        return pltpu.make_async_copy(saved_hbm[name], saved[name], saved_sem.at[SAVED.index(name)])
+
+    loads = [
+        pltpu.make_async_copy(src, dst, load_sem.at[i])
+        for i, (src, dst) in enumerate(zip([x_hbm, shift_hbm, cot_hbm, *weights_hbm], [x, shift, cot, *weights]))
+    ]
+    first = (HAT_B3, OUT_A)
+    for name in first:
+        loading(name).start()
+    loads[2].start()
+    order = (HAT_B2, ACT_B2, HAT_B1, PATCH_B, HAT_A3, HAT_AS, HAT_A2, ACT_A2, HAT_A1)
+    loads[9].start()
+    for name in order[:4]:
+        loading(name).start()
+    for i in (1, 8, 7):
+        loads[i].start()
+    for name in order[4:]:
+        loading(name).start()
+    for i in (5, 6, 4, 0, 3):
+        loads[i].start()
+
+    greet(depth)
+
+    def quarter(d):
+        return pl.ds(pl.multiple_of(d * 256, 256), 256)
+
+    def affine(hat, params, row, at):
+        return hat[:, at].astype(jnp.float32) * params[row : row + 1, at] + params[row + 1 : row + 2, at]
+
+    def norm_back(dz_of, hat, total, base, inverse, params, row, target, blocks):
+        def body(j, carry):
+            at = columns(j)
+            sums_at = columns(base + j)
+            gain = params[row : row + 1, at]
+            value, xhat = dz_of(j), hat[:, at].astype(jnp.float32)
+
+            def of(g, span):
+                first = total[g : g + 1, sums_at] * over_of(g)
+                second = total[3 + g : 4 + g, sums_at] * over_of(g)
+                return (gain * inverse[g : g + 1, at]) * (value[span] - first - xhat[span] * second)
+
+            target[:, at] = (by_group(plan, of) * mask[...]).astype(jnp.bfloat16)
+            return carry
+
+        lax.fori_loop(0, blocks, body, 0)
+
+    scale = [1.0]
+
+    def over_of(g):
+        return over[g : g + 1, :] * scale[0]
+
+    for name in first:
+        loading(name).wait()
+    loads[2].wait()
+
+    def out_pairs(j):
+        at = columns(j)
+        v = affine(saved[HAT_B3], par_out, 4, at) + saved[OUT_A][:, at].astype(jnp.float32)
+        value = cot[:, at].astype(jnp.float32) * mask[...] * slope(v)
+        dz[:, at] = value
+        return [(value, saved[HAT_B3][:, at].astype(jnp.float32))]
+
+    total = sums[SUM_B3]
+    put_sums(plan, out_pairs, mask, total.pay, 0, 2048)
+    total.begin()
+    for i in (9, 1, 8, 7):
+        loads[i].wait()
+    for name in order[:4]:
+        loading(name).wait()
+    flip[0:512] = saved[ACT_B2][...].T
+    interleave(total.stages(), [])
+    pgrad_b3[...] = total.total[...]
+    norm_back(lambda j: dz[:, columns(j)], saved[HAT_B3], total.total, 0, inv_out.at[2], par_out, 4, dh_a, 16)
+
+    def contract(dh, weight):
+        dact[...] = dot_nt(dh[:, 0:256], weight[0, 0].reshape(512, 256))
+
+        def body(d, carry):
+            dact[...] += dot_nt(dh[:, quarter(d)], weight[d // 2, lax.rem(d, 2)].reshape(512, 256))
+            return carry
+
+        lax.fori_loop(1, 8, body, 0)
+
+    def expand_term(lhs, dh, weight, first_slot, last_slot):
+        def body(d, carry):
+            shape = weight.shape[2:]
+            weight[d // 2, lax.rem(d, 2)] = dot(lhs, dh[:, quarter(d)]).astype(jnp.bfloat16).reshape(shape)
+            return carry
+
+        lax.fori_loop(first_slot, last_slot, body, 0)
+
+    def mid_pairs(hat, row):
+        def pairs(j):
+            at = columns(j)
+            value = dact[:, at] * slope(affine(saved[hat], par_mid, row, at))
+            dact[:, at] = value
+            return [(value, saved[hat][:, at].astype(jnp.float32))]
+
+        return pairs
+
+    def mid_norm(name, hat, index, row, works):
+        total = sums[name]
+        put_sums(plan, mid_pairs(hat, row), mask, total.pay, 0, 512)
+        total.begin()
+        interleave(total.stages(), works)
+        pgrad_mid[index] = total.total[...]
+        norm_back(lambda j: dact[:, columns(j)], saved[hat], total.total, 0, inv_mid.at[index], par_mid, row, dh_mid, 4)
+
+    contract(dh_a, w_b3)
+
+    def third_term(part):
+        def work():
+            expand_term(flip[0:512, :], dh_a, w_b3, 4 * part, 4 * part + 4)
+            if part:
+                reduce.enable(6)
+                pump()
+
+        return work
+
+    mid_norm(SUM_B2, HAT_B2, 3, 6, [third_term(0), third_term(1)])
+
+    def spread(tap, carry):
+        part = dot(
+            dot(shift[8 - tap], dh_mid[...]).astype(jnp.bfloat16), w_b2[:, :, tap].reshape(512, 512)
+        )
+        dact[...] = part + jnp.where(tap == 0, 0.0, dact[...])
+        return carry
+
+    lax.fori_loop(0, 3, spread, 0)
+    pump()
+    lax.fori_loop(3, 6, spread, 0)
+    pump()
+    lax.fori_loop(6, 9, spread, 0)
+    flip[0:512] = dh_mid[...].T
+
+    def spatial_term(weight, patch, first_tap, last_tap, tensor):
+        def work():
+            def body(tap, carry):
+                weight[:, :, tap] = dot(flip[0:512, :], patch[tap]).astype(jnp.bfloat16).reshape(depth, 2, 64, 512)
+                return carry
+
+            lax.fori_loop(first_tap, last_tap, body, 0)
+            reduce.enable(tensor, last_tap)
+            pump()
+
+        return work
+
+    mid_norm(
+        SUM_B1,
+        HAT_B1,
+        2,
+        4,
+        [spatial_term(w_b2, saved[PATCH_B], 0, 3, 5), spatial_term(w_b2, saved[PATCH_B], 3, 6, 5)],
+    )
+    spatial_term(w_b2, saved[PATCH_B], 6, 9, 5)()
+    loading(PATCH_A).start()
+
+    def residual(d, carry):
+        at = quarter(d)
+        dz[:, at] = dz[:, at] + dot(dh_mid[...], w_b1[:, :, 0, :, at].reshape(512, 256))
+        return carry
+
+    lax.fori_loop(0, 4, residual, 0)
+    pump()
+    lax.fori_loop(4, 8, residual, 0)
+    pump()
+    for name in order[4:]:
+        loading(name).wait()
+
+    def join_pairs(j):
+        at = columns(j)
+        v = affine(saved[HAT_A3], par_out, 0, at) + affine(saved[HAT_AS], par_out, 2, at)
+        value = dz[:, at] * mask[...] * slope(v)
+        dz[:, at] = value
+        return [(value, saved[HAT_A3][:, at].astype(jnp.float32))]
+
+    total = sums[SUM_J]
+    put_sums(plan, join_pairs, mask, total.pay, 0, 2048)
+    put_sums(
+        plan, lambda j: [(dz[:, columns(j)], saved[HAT_AS][:, columns(j)].astype(jnp.float32))], mask, total.pay, 16, 2048
+    )
+    total.begin()
+    flip[0:512] = dh_mid[...].T
+
+    def first_term(part):
+        def work():
+            def body(d, carry):
+                at = quarter(d)
+                value = dot(flip[0:512, :], saved[OUT_A][:, at]).astype(jnp.bfloat16)
+                w_b1[:, :, 0, :, at] = value.reshape(depth, 2, 64, 256)
+                return carry
+
+            lax.fori_loop(2 * part, 2 * part + 2, body, 0)
+            if part == 3:
+                reduce.enable(4)
+            pump()
+
+        return work
+
+    interleave(total.stages(), [first_term(part) for part in range(4)])
+    pgrad_j[...] = total.total[...]
+    norm_back(lambda j: dz[:, columns(j)], saved[HAT_A3], total.total, 0, inv_out.at[0], par_out, 0, dh_a, 16)
+    pump()
+    norm_back(lambda j: dz[:, columns(j)], saved[HAT_AS], total.total, 16, inv_out.at[1], par_out, 2, dh_b, 16)
+    for i in (5, 6, 4, 0, 3):
+        loads[i].wait()
+
+    pump()
+    contract(dh_a, w_a3)
+    pump()
+    flip[0:512] = saved[ACT_A2][...].T
+
+    def third_term_a():
+        expand_term(flip[0:512, :], dh_a, w_a3, 0, 8)
+        reduce.enable(2)
+        pump()
+
+    def shortcut():
+        even = dz.at[:, 0:1024]
+        even[...] = dot_nt(dh_b[:, 0:256], w_as[0, 0].reshape(1024, 256))
+
+        def body(d, carry):
+            even[...] += dot_nt(dh_b[:, quarter(d)], w_as[d // 2, lax.rem(d, 2)].reshape(1024, 256))
+            return carry
+
+        lax.fori_loop(1, 8, body, 0)
+
+        def keep(j, carry):
+            value = even[:, columns(j)]
+            high = value.astype(jnp.bfloat16)
+            saved[OUT_A][:, columns(j)] = high
+            saved[OUT_A][:, columns(8 + j)] = (value - high.astype(jnp.float32)).astype(jnp.bfloat16)
+            return carry
+
+        lax.fori_loop(0, 8, keep, 0)
+
+    mid_norm(SUM_A2, HAT_A2, 1, 2, [third_term_a, shortcut])
+
+    loading(PATCH_A).wait()
+    flip[...] = x[0].T
+    expand_term(flip[...], dh_b, w_as, 0, 8)
+    reduce.enable(3)
+    for plane in range(4):
+        at = slice(plane * 512, plane * 512 + 512)
+        begun = False
+        for tap in range(9):
+            a, b = tap // 3, tap % 3
+            if plane != (0 if a == 1 else 2) + (0 if b == 1 else 1):
+                continue
+            matrix = (2 if a == 0 else 1) * 3 + (2 if b == 0 else 1)
+            moved = dh_mid[...] if matrix == 4 else dot(shift[matrix], dh_mid[...]).astype(jnp.bfloat16)
+            part = dot(moved, w_a2[:, :, tap].reshape(512, 512))
+            if begun:
+                dz[:, at] += part
+            else:
+                dz[:, at] = part
+            begun = True
+        pump()
+
+    def plane_pairs(j):
+        at = columns(j)
+        pairs = []
+        for plane in range(4):
+            wide = columns(4 * plane + j)
+            xhat = saved[HAT_A1][plane, :, at].astype(jnp.float32)
+            v = xhat * par_mid[0:1, at] + par_mid[1:2, at]
+            value = dz[:, wide] * slope(v)
+            dz[:, wide] = value
+            pairs.append((value, xhat))
+        return pairs
+
+    total = sums[SUM_A1]
+    put_sums(plan, plane_pairs, mask, total.pay, 0, 512)
+    total.begin()
+    flip[0:512] = dh_mid[...].T
+    stages = total.stages()
+    spatial_term(w_a2, saved[PATCH_A], 0, 3, 1)()
+    stages[0]()
+    spatial_term(w_a2, saved[PATCH_A], 3, 6, 1)()
+    stages[1]()
+    spatial_term(w_a2, saved[PATCH_A], 6, 9, 1)()
+    pgrad_mid[0] = total.total[...]
+    scale[0] = 0.25
+    for plane in range(4):
+        norm_back(
+            lambda j, plane=plane: dz[:, columns(4 * plane + j)],
+            saved[HAT_A1].at[plane],
+            total.total,
+            0,
+            inv_mid.at[0],
+            par_mid,
+            0,
+            planes[plane],
+            4,
+        )
+
+    def input_gradient(p):
+        target = (dh_a if p < 2 else dh_b).at[:, pl.ds((p % 2) * 1024, 1024)]
+        value = dot(planes[p][...], w_a1[...].reshape(512, -1))
+        if p == 0:
+            value = value + saved[OUT_A][:, 0:1024].astype(jnp.float32)
+            value = value + saved[OUT_A][:, 1024:2048].astype(jnp.float32)
+        target[...] = value.astype(jnp.bfloat16)
+        copy = pltpu.make_async_copy(target, dx_hbm.at[p], dx_sem.at[p])
+        copy.start()
+        return copy
+
+    copies = []
+    for p in range(4):
+        copies.append(input_gradient(p))
+        pump()
+
+    def last_term(c, carry):
+        at = quarter(c)
+        total = jnp.zeros((512, 256), jnp.float32)
+        for p in range(4):
+            total = total + lax.dot_general(
+                planes[p][...], x[p, :, at], (((0,), (0,)), ((), ())), preferred_element_type=jnp.float32
+            )
+        w_a1[:, :, 0, :, at] = total.astype(jnp.bfloat16).reshape(depth, 2, 64, 256)
+        return carry
+
+    lax.fori_loop(0, 4, last_term, 0)
+    reduce.enable(0)
+    reduce.finish(weight_squares, squares_out)
+    for copy in copies:
+        copy.wait()
+    for total in sums.values():
+        total.close()
+
+
+def run_backward(plan, depth, x, shifts, cot, mask, weight_squares, small, saved, fulls):
+    rows, f32, bf16 = plan.rows, jnp.float32, jnp.bfloat16
+    dma = pltpu.SemaphoreType.DMA
+    scratch = []
+    for _, pieces in backward_names(depth):
+        scratch += pieces
+    scratch += [pltpu.VMEM(value.shape, bf16) for value in (x, shifts, cot)]
+    scratch += [pltpu.VMEM(full.shape, bf16) for full in fulls]
+    scratch += [pltpu.VMEM(shape, kind) for name, (shape, kind) in zip(SAVED, saved_shapes(rows)) if name != PATCH_B]
+    scratch += [
+        pltpu.VMEM((rows, 2048), f32),
+        pltpu.VMEM((rows, 512), f32),
+        pltpu.VMEM((rows, 512), bf16),
+        pltpu.VMEM((1024, rows), bf16),
+        dma((10,)),
+        dma((len(SAVED),)),
+        dma((4,)),
+    ]
+    shapes = [full.shape for full in fulls]
+    scratch += Reduce.scratch(shapes, depth)
+
+    def part(shape, over):
+        return jax.ShapeDtypeStruct((*shape[:3], shape[3] // over, shape[4]), bf16)
+
+    outs = pl.pallas_call(
+        functools.partial(backward_kernel, plan, depth),
+        out_shape=[
+            jax.ShapeDtypeStruct(x.shape, bf16),
+            jax.ShapeDtypeStruct((4, 8, 512), f32),
+            jax.ShapeDtypeStruct((8, 2048), f32),
+            jax.ShapeDtypeStruct((8, 4096), f32),
+            jax.ShapeDtypeStruct((8, 128), f32),
+        ]
+        + [jax.ShapeDtypeStruct(shape[2:], bf16) for shape in shapes]
+        + [part(shape, 2) for shape in shapes]
+        + [part(shape, 4) for shape in shapes],
+        in_specs=[ANY] * 3 + [WHOLE] * 7 + [ANY] * len(SAVED) + [ANY] * 7,
+        out_specs=[ANY] + [WHOLE] * 4 + [ANY] * 21,
+        scratch_shapes=scratch,
+        compiler_params=pltpu.CompilerParams(collective_id=1, has_side_effects=True, vmem_limit_bytes=VMEM_LIMIT),
+    )(x, shifts, cot, mask, weight_squares, *small, *saved, *fulls)
+    return outs[:12]
+
+
+def on_device(
+    input_160,
+    input_224,
+    input_288,
+    cotangent_160,
+    cotangent_224,
+    cotangent_288,
+    live_counts,
+    conv_a1,
+    norm_a1,
+    conv_a2,
+    norm_a2,
+    conv_a3,
+    norm_a3,
+    conv_as,
+    norm_as,
+    conv_b1,
+    norm_b1,
+    conv_b2,
+    norm_b2,
+    conv_b3,
+    norm_b3,
+):
+    if conv_a1.shape[1] % 64 or conv_a3.shape[1] % 128 or lax.axis_size(REP) != 4:
+        return plain_on_device(
+            input_160,
+            input_224,
+            input_288,
+            cotangent_160,
+            cotangent_224,
+            cotangent_288,
+            live_counts,
+            conv_a1,
+            norm_a1,
+            conv_a2,
+            norm_a2,
+            conv_a3,
+            norm_a3,
+            conv_as,
+            norm_as,
+            conv_b1,
+            norm_b1,
+            conv_b2,
+            norm_b2,
+            conv_b3,
+            norm_b3,
+        )
+    depth = lax.axis_size(DP) // 2
+    inputs = (input_160, input_224, input_288)
+    plan = Plan([value.shape for value in inputs])
+    shards = (
+        conv_a1.T[None],
+        jnp.transpose(conv_a2, (0, 1, 3, 2)).reshape(9, conv_a2.shape[3], conv_a2.shape[2]),
+        conv_a3.reshape(2, -1, conv_a3.shape[1]),
+        conv_as.reshape(4, -1, conv_as.shape[1]),
+        conv_b1.T[None],
+        jnp.transpose(conv_b2, (0, 1, 3, 2)).reshape(9, conv_b2.shape[3], conv_b2.shape[2]),
+        conv_b3.reshape(2, -1, conv_b3.shape[1]),
+    )
+    local_weights = (conv_a1, conv_a2, conv_a3, conv_as, conv_b1, conv_b2, conv_b3)
+
+    planes, cotangents, masks, live_pixels = [], [], [], []
+    for g, (value, cotangent) in enumerate(
+        zip(inputs, (cotangent_160, cotangent_224, cotangent_288))
+    ):
+        side, slots, fill = plan.sides[g], plan.slots[g], plan.sizes[g] - plan.valid[g]
+        split = jnp.transpose(value, (1, 2, 0, 3)).reshape(side, 2, side, 2, slots, -1)
+        split = jnp.transpose(split, (1, 3, 0, 2, 4, 5)).reshape(4, plan.valid[g], -1)
+        planes.append(jnp.pad(split, ((0, 0), (0, fill), (0, 0))))
+        cotangents.append(
+            jnp.pad(jnp.transpose(cotangent, (1, 2, 0, 3)).reshape(plan.valid[g], -1), ((0, fill), (0, 0)))
+        )
+        row = jnp.arange(plan.sizes[g])
+        live = (lax.rem(row, slots) < live_counts[0, g]) & (row < plan.valid[g])
+        masks.append(jnp.broadcast_to(live.astype(jnp.float32)[:, None], (plan.sizes[g], 128)))
+        live_pixels.append((live_counts[0, g] * (side * side)).astype(jnp.float32))
+    x = jnp.concatenate(planes, axis=1)
+    cot = jnp.concatenate(cotangents, axis=0)
+    mask = jnp.concatenate(masks, axis=0)
+    counts = jnp.pad(jnp.stack(live_pixels), (0, 125)).reshape(1, 128)
+
+    def own_place(norms, width):
+        rows = jnp.concatenate(norms, axis=0).astype(jnp.float32)
+        rows = jnp.pad(rows, ((0, 8 - rows.shape[0]), (0, 0)))
+        rows = jnp.where(lax.axis_index(REP) == 0, rows, 0.0)
+        start = lax.axis_index(DP) * rows.shape[1]
+        return lax.dynamic_update_slice(jnp.zeros((8, width), jnp.float32), rows, (0, start))
+
+    mid_local, out_local = norm_a1.shape[1], norm_a3.shape[1]
+    mid_width, out_width = mid_local * 2 * depth, out_local * 2 * depth
+    norm_mid = own_place((norm_a1, norm_a2, norm_b1, norm_b2), mid_width)
+    norm_out = own_place((norm_a3, norm_as, norm_b3), out_width)
+    shifts = jnp.asarray(plan.shifts())
+
+    out, *results = run_forward(plan, depth, x, shifts, mask, counts, norm_mid, norm_out, shards)
+    small, fulls, saved = results[:5], results[5:12], results[12:]
+    square_row = jnp.stack([jnp.sum(jnp.square(weight.astype(jnp.float32))) for weight in local_weights])
+    square_row = jnp.pad(square_row.reshape(1, 7), ((0, 7), (0, 121)))
+    dx, pgrad_mid, pgrad_b3, pgrad_j, squares, *totals = run_backward(
+        plan, depth, x, shifts, cot, mask, square_row, small, saved, fulls
+    )
+
+    def spatial_out(total):
+        return jnp.transpose(total, (0, 2, 1)).reshape(conv_a2.shape).astype(jnp.float32)
+
+    gradients = (
+        totals[0][0].T.astype(jnp.float32),
+        spatial_out(totals[1]),
+        totals[2].reshape(conv_a3.shape).astype(jnp.float32),
+        totals[3].reshape(conv_as.shape).astype(jnp.float32),
+        totals[4][0].T.astype(jnp.float32),
+        spatial_out(totals[5]),
+        totals[6].reshape(conv_b3.shape).astype(jnp.float32),
+    )
+
+    def norm_gradient(sums, local):
+        both = jnp.stack([sums[3] + sums[4] + sums[5], sums[0] + sums[1] + sums[2]])
+        return lax.dynamic_slice_in_dim(both, lax.axis_index(DP) * local, local, 1)
+
+    norm_gradients = (
+        norm_gradient(pgrad_mid[0], mid_local),
+        norm_gradient(pgrad_mid[1], mid_local),
+        norm_gradient(pgrad_j[:, :out_width], out_local),
+        norm_gradient(pgrad_j[:, out_width:], out_local),
+        norm_gradient(pgrad_mid[2], mid_local),
+        norm_gradient(pgrad_mid[3], mid_local),
+        norm_gradient(pgrad_b3, out_local),
+    )
+    weight_totals, grad_totals = squares[0, :7], squares[1, :7]
+    weight_norm = jnp.sqrt(weight_totals)
+    grad_norm = jnp.sqrt(grad_totals)
+    trust_ratio = weight_norm / (grad_norm + DECAY_RATE * weight_norm)
+    scaled = [
+        trust_ratio[i] * (gradients[i] + DECAY_RATE * local_weights[i].astype(jnp.float32)) for i in range(7)
+    ]
+    outputs, grad_inputs = [], []
+    for g in range(3):
+        side, slots, start = plan.sides[g], plan.slots[g], plan.starts[g]
+        rows = out[start : start + plan.valid[g]].reshape(side, side, slots, -1)
+        outputs.append(jnp.transpose(rows, (2, 0, 1, 3)))
+        split = dx[:, start : start + plan.valid[g]].reshape(2, 2, side, side, slots, -1)
+        split = jnp.transpose(split, (2, 0, 3, 1, 4, 5)).reshape(2 * side, 2 * side, slots, -1)
+        grad_inputs.append(jnp.transpose(split, (2, 0, 1, 3)))
+    pairs = [piece for pair in zip(gradients, norm_gradients) for piece in pair]
+    return (*outputs, *grad_inputs, *pairs, *scaled, jnp.stack([weight_totals, grad_totals]))
+
+
 def solution(mesh):
-    placed = (
-        P(("dp", "rep"), None, None, None),
-        P(("dp", "rep"), None, None, None),
-        P(("dp", "rep"), None, None, None),
-        P(("dp", "rep"), None, None, None),
-        P(("dp", "rep"), None, None, None),
-        P(("dp", "rep"), None, None, None),
-        P(("dp", "rep"), None),
-        P(None, "dp"),
-        P(None, "dp"),
-        P(None, None, None, "dp"),
-        P(None, "dp"),
-        P(None, "dp"),
-        P(None, "dp"),
-        P(None, "dp"),
-        P(None, "dp"),
-        P(None, "dp"),
-        P(None, "dp"),
-        P(None, None, None, "dp"),
-        P(None, "dp"),
-        P(None, "dp"),
-        P(None, "dp"),
-    )
+    by_image, by_column = P((DP, REP), None, None, None), P(None, DP)
+    by_channel = P(None, None, None, DP)
+    weights = [by_column, by_column, by_channel] + [by_column] * 7 + [by_channel] + [by_column] * 3
+    kernels = [by_column, by_channel] + [by_column] * 3 + [by_channel, by_column]
     return jax.shard_map(
         on_device,
         mesh=mesh,
-        in_specs=placed,
-        out_specs=(
-            P(("dp", "rep"), None, None, None),
-            P(("dp", "rep"), None, None, None),
-            P(("dp", "rep"), None, None, None),
-            P(("dp", "rep"), None, None, None),
-            P(("dp", "rep"), None, None, None),
-            P(("dp", "rep"), None, None, None),
-            P(None, "dp"),
-            P(None, "dp"),
-            P(None, None, None, "dp"),
-            P(None, "dp"),
-            P(None, "dp"),
-            P(None, "dp"),
-            P(None, "dp"),
-            P(None, "dp"),
-            P(None, "dp"),
-            P(None, "dp"),
-            P(None, None, None, "dp"),
-            P(None, "dp"),
-            P(None, "dp"),
-            P(None, "dp"),
-            P(None, "dp"),
-            P(None, None, None, "dp"),
-            P(None, "dp"),
-            P(None, "dp"),
-            P(None, "dp"),
-            P(None, None, None, "dp"),
-            P(None, "dp"),
-            P(),
-        ),
+        in_specs=(*[by_image] * 6, P((DP, REP), None), *weights),
+        out_specs=(*[by_image] * 6, *weights, *kernels, P()),
         check_vma=False,
     )

time: 2340 us -> 484 us (0.21)
  waiting for transfers between devices: 912 us -> 0 us
  blocking collectives: 565 us -> 0 us
  Pallas kernels: 0 us -> 401 us
  other arithmetic: 335 us -> 29.1 us
  local copies, waits for them, and re-layouts: 331 us -> 42.1 us
  matrix products: 157 us -> 0 us
    reduce_scatter x7 -> x0, waiting for transfers between devices: 682 us -> none  [the longest x1 164 us: on_device(): lax.psum_scatter(term_b2, 'dp', scatter_dimension=3, tiled=True)]
    psum x11 -> x0, blocking collectives: 438 us -> none  [the longest x5 212 us: batch_norm(): lax.psum((firsts[0], seconds[0], firsts[1], seconds[1], firsts[2], second...]
    pallas_call x0 -> x2, Pallas kernels: none -> 401 us  [the longest x1 222 us: run_backward(): pl.pallas_call(functools.partial(backward_kernel, plan, depth), out_shape...]
    psum x3 -> x0, waiting for transfers between devices: 185 us -> none  [the longest x1 123 us: norm_back(): lax.psum((firsts[0], seconds[0], firsts[1], seconds[1], firsts[2], second...]
    dot_general x63 -> x0, matrix products: 157 us -> none  [the longest x21 61.4 us: weight_term(): jnp.einsum('nhwc,nhwd->cd', inputs, upstream, preferred_element_type=jnp....]
    scatter-add x30 -> x0, other arithmetic: 143 us -> none  [the longest x27 122 us: fold_patches(): padded = padded.at[:, offset_row:offset_row + side_in:stride, offset_col:...]
    slice x74 -> x8, local copies, waits for them, and re-layouts: 135 us -> 6.3 us  [the longest x3 3.87 us: on_device(): dx[:, start:start + plan.valid[g]].reshape(2, 2, side, side, slots, -1)]
    all_gather x7 -> x0, blocking collectives: 127 us -> none  [the longest x1 22.1 us: on_device(): lax.all_gather(norm_a1, 'dp', axis=1, tiled=True)]
  transfers between devices with their start and end apart: 17 -> 0, of which waited for: 10 -> 0; matrix products, arithmetic and copies ran while one was open for 17% -> 0% of each run, Pallas kernels for 0% -> 0%
where the time goes in v1:
time: 484 us; the launch traced here: 475 us
  Pallas kernels  401 us (83%)
  local copies, waits for them, and re-layouts  42.1 us (9%)
  other arithmetic  29.1 us (6%)
    pallas_call x1, Pallas kernels, run_backward(): pl.pallas_call(functools.partial(backward_kernel, plan, depth), out_shape...  222 us
    pallas_call x1, Pallas kernels, run_forward(): pl.pallas_call(functools.partial(forward_kernel, plan, depth), out_shape=...  178 us
    mul x7, other arithmetic, on_device(): trust_ratio[i]  12.7 us

profile of v1, /device:TPU:0, one launch (start us, length us, event | category | flops | bytes accessed | tf_op | source)
XLA Modules:
  0.0 475.5 jit_solution(7321208437862891338)
XLA Ops:
  0.7 3.3 copy.74
  4.0 1.7 reshape.464
  5.7 0.8 copy.76
  6.5 0.3 reshape.462
  6.9 0.2 copy.63
  7.1 0.9 copy-done.13
  8.0 1.2 copy.75
  9.2 1.6 reshape.460
  10.9 1.9 fusion.5.refs_0_
  12.8 0.6 fusion.48
  13.4 0.6 and_convert_fusion
  14.0 1.3 and_convert_fusion.1
  15.4 0.8 broadcast.82.refs_2_.refs_3_
  18.2 0.6 fusion.45.refs_3_
  18.8 0.3 dynamic_update_slice.6.refs_4_
  19.2 0.5 copy-done.27
  19.7 0.1 copy-done.21
  19.8 178.5 %shard_map.429 = (bf16[384,2048]{1,0:T(8,128)(2,1)}, f32[4,8,512]{2,1,0:T(8,128)}, f32[3,8,2048]{2,1,0:T(8,128)}, f32[8,512]{1,0:T(8,128)}, f32[8,2048]{1,0:T(8,...) custom-call(bf16[4,384,1024]{2,1,0:T(8,128)(2,1)} %fusion.5.refs_0_,, ...), custom_call_target="tpu_custom_call" | custom-call | tf_op jit(solution)/shard_map/pallas_call | solution.py:1547
  198.3 1.2 slice.253
  199.4 0.9 reshape.471
  200.4 1.0 reshape.472
  201.5 1.3 reshape.473
  202.8 0.3 reshape.476
  203.1 0.7 copy-done.20
  203.8 0.2 reshape.475
  204.0 0.1 reshape.474
  204.1 1.3 fusion.11.refs_2_
  205.4 0.7 fusion.30
  206.1 0.9 fusion.12
  207.0 0.7 fusion.21
  207.8 0.9 fusion.18
  208.6 0.7 fusion.24
  209.4 0.9 fusion.15
  210.3 0.7 fusion.27
  211.0 4.6 stack.85
  215.6 0.6 pad.48.refs_4_
  216.2 222.3 %shard_map.430 = (bf16[4,384,1024]{2,1,0:T(8,128)(2,1)}, f32[4,8,512]{2,1,0:T(8,128)}, f32[8,2048]{1,0:T(8,128)}, f32[8,4096]{1,0:T(8,128)}, f32[8,128]{1,0:T(8,...) custom-call(bf16[4,384,1024]{2,1,0:T(8,128)(2,1)} %fusion.5.refs_0_,, ...), custom_call_target="tpu_custom_call" | custom-call | tf_op jit(solution)/shard_map/pallas_call | solution.py:1955
  438.5 1.2 slice.256
  439.8 1.3 reshape.478
  441.0 2.5 copy.65
  443.5 1.2 slice.257
  444.8 1.5 reshape.491
  446.2 2.7 copy.67
  449.0 1.4 slice.258
  450.4 1.8 reshape.482
  452.2 3.7 copy.68
  456.0 0.6 fusion.47
  456.6 1.5 fusion.32
  458.1 0.6 fusion.44
  458.8 0.1 convert_element_type.174
  459.0 0.6 fusion.43
  459.6 1.7 fusion.23
  461.4 0.7 fusion.40
  462.0 2.2 fusion.20
  464.3 0.7 fusion.39
  464.9 1.8 fusion.26
  466.7 0.6 fusion.42
  467.4 0.1 convert_element_type.176
  467.5 0.7 fusion.41
  468.3 1.7 fusion.29
  470.0 0.7 fusion.38
  470.7 1.9 fusion.14
  472.6 1.9 fusion.17
  474.5 0.6 stack.93
  (86 shorter events, 0.5 us)
Async XLA Ops:
  4.0 1.7 copy-start.14
  6.9 1.1 copy-start.13
  10.8 2.0 copy-start.30
  10.8 7.9 %copy-start.34 = (bf16[2,64]{1,0:T(2,128)(2,1)S(1)}, bf16[2,64]{1,0:T(2,128)(2,1)}, u32[]{:S(2)}) copy-start(bf16[2,64]{1,0:T(2,128)(2,1)} %param.40) | copy-start | bytes 772
  10.8 7.9 %copy-start.35 = (bf16[2,64]{1,0:T(2,128)(2,1)S(1)}, bf16[2,64]{1,0:T(2,128)(2,1)}, u32[]{:S(2)}) copy-start(bf16[2,64]{1,0:T(2,128)(2,1)} %param.38) | copy-start | bytes 772
  10.8 7.9 %copy-start.36 = (bf16[2,64]{1,0:T(2,128)(2,1)S(1)}, bf16[2,64]{1,0:T(2,128)(2,1)}, u32[]{:S(2)}) copy-start(bf16[2,64]{1,0:T(2,128)(2,1)} %param.32) | copy-start | bytes 772
  10.9 7.9 %copy-start.37 = (bf16[2,64]{1,0:T(2,128)(2,1)S(1)}, bf16[2,64]{1,0:T(2,128)(2,1)}, u32[]{:S(2)}) copy-start(bf16[2,64]{1,0:T(2,128)(2,1)} %param.30) | copy-start | bytes 772
  10.9 8.2 %copy-start.31 = (bf16[2,256]{1,0:T(2,128)(2,1)S(1)}, bf16[2,256]{1,0:T(2,128)(2,1)}, u32[]{:S(2)}) copy-start(bf16[2,256]{1,0:T(2,128)(2,1)} %param.42) | copy-start | bytes 3076
  10.9 8.2 %copy-start.32 = (bf16[2,256]{1,0:T(2,128)(2,1)S(1)}, bf16[2,256]{1,0:T(2,128)(2,1)}, u32[]{:S(2)}) copy-start(bf16[2,256]{1,0:T(2,128)(2,1)} %param.36) | copy-start | bytes 3076
  10.9 8.2 %copy-start.33 = (bf16[2,256]{1,0:T(2,128)(2,1)S(1)}, bf16[2,256]{1,0:T(2,128)(2,1)}, u32[]{:S(2)}) copy-start(bf16[2,256]{1,0:T(2,128)(2,1)} %param.34) | copy-start | bytes 3076
  19.1 0.6 copy-start.27
  19.1 0.6 copy-start.21
  198.3 2.1 copy-start.10
  201.4 1.4 copy-start.15
  201.5 2.5 copy-start.19
  202.8 1.0 copy-start.20
  204.1 1.4 copy-start.11
  204.1 2.0 copy-start
  204.1 2.9 copy-start.5
  204.1 3.6 copy-start.4
  204.1 4.5 copy-start.6
  205.4 3.9 copy-start.1
  205.4 4.8 %copy-start.8 = (bf16[512,256]{1,0:T(8,128)(2,1)S(1)}, bf16[512,256]{1,0:T(8,128)(2,1)}, u32[]{:S(2)}) copy-start(bf16[512,256]{1,0:T(8,128)(2,1)} %param.41) | copy-start | bytes 786436
  452.2 3.8 copy-start.38
  452.2 4.4 copy-start.12
  452.2 4.4 copy-start.25
  452.2 5.9 %copy-start.29 = (f32[4,8,512]{2,1,0:T(8,128)S(1)}, f32[4,8,512]{2,1,0:T(8,128)}, u32[]{:S(2)}) copy-start(f32[4,8,512]{2,1,0:T(8,128)} %get-tuple-element.92) | copy-start | bytes 196612
  452.2 6.5 %copy-start.17 = (bf16[9,64,512]{2,1,0:T(8,128)(2,1)S(1)}, bf16[9,64,512]{2,1,0:T(8,128)(2,1)}, u32[]{:S(2)}) copy-start(bf16[9,64,512]{2,1,0:T(8,128)(2,1)} %get-tuple-element.93) | copy-start | bytes 1769476
  456.0 3.6 copy-start.24
  458.8 2.5 copy-start.26
  458.8 3.3 copy-start.18
  458.9 11.8 %copy-start.2 = (f32[9,64,512]{2,1,0:T(8,128)}, f32[9,64,512]{2,1,0:T(8,128)S(1)}, u32[]{:S(2)}) copy-start(f32[9,64,512]{2,1,0:T(8,128)S(1)} %convert_element_type.174) | copy-start | bytes 3538948
  462.0 2.9 copy-start.7
  462.0 2.9 copy-start.23
  464.3 3.1 copy-start.16
  464.9 3.3 copy-start.9
  464.9 3.3 copy-start.22
  467.3 2.6 copy-start.28
  467.5 5.1 %copy-start.3 = (f32[9,64,512]{2,1,0:T(8,128)}, f32[9,64,512]{2,1,0:T(8,128)S(1)}, u32[]{:S(2)}) copy-start(f32[9,64,512]{2,1,0:T(8,128)S(1)} %convert_element_type.176) | copy-start | bytes 3538948
